TPU v7x, 128 devices: a whole 4x4x4 slice. The times are simulated.
128 devices in a mesh: seq: 16 (over z, y), head: 8 (over x, core).
Axes of the slice: x: 4, y: 4, z: 4, core: 2. Of those that a mesh axis runs over, the one named last changes fastest.
Arguments:
- qkv: bfloat16 [16384, 3, 3072], P(('seq', 'head')), may hold values from -6 to 6
- eta: float32 [48], P('head'), may hold values from 1.8310548e-05 to 0.00390625
- initial: float32 [48, 64, 64], P('head'), may hold values from -0.75 to 0.75
- gain: float32 [3072], P('head'), may hold values from 0.25 to 1.75
- w_out: bfloat16 [3072, 3072], P('head'), may hold values from -0.109375 to 0.109375
Outputs:
- mixed: float32 [16384, 3072], P(('seq', 'head'))
All inputs are finite; a program needn't handle non-finite values.
Results may differ from a plain program's by a relative error of at most 0.0029.
Values may be sent and summed in bfloat16 or wider, within the bound.
A program may use at most 128 MiB of HBM per device.

v0:
```python
import jax
import jax.numpy as jnp
from jax import lax
from jax.sharding import PartitionSpec as P

MB = 64


precise = lax.Precision.HIGHEST


def prefix(value, axis, combine, identity, reverse):
    peers, place = (lax.axis_size(axis), lax.axis_index(axis))
    everything = jax.tree.map(lambda part: lax.all_gather(part, axis), value)
    start = jax.tree.map(
        lambda part, zero: jnp.broadcast_to(jnp.asarray(zero, part.dtype), part.shape),
        value,
        identity,
    )

    def hop(k, before):
        at = peers - 1 - k if reverse else k
        reached = at > place if reverse else at < place
        new = combine(before, jax.tree.map(lambda part: part[at], everything))
        return jax.tree.map(lambda a, b: jnp.where(reached, a, b), new, before)

    return lax.fori_loop(0, peers, hop, start)


def apply_map(affine, fast_state):
    return jnp.einsum("hij,hjk->hik", affine[0], fast_state, precision=precise) + affine[1]


def compose(earlier, later):
    linear = jnp.einsum("hij,hjk->hik", later[0], earlier[0], precision=precise)
    offset = jnp.einsum("hij,hjk->hik", later[0], earlier[1], precision=precise) + later[1]
    return (linear, offset)


def shards(qkv, eta, initial, gain, w_out):
    head_major = lax.all_to_all(qkv, "head", split_axis=2, concat_axis=0, tiled=True)
    seq_rows = head_major.shape[0]
    head_count = initial.shape[0]
    head_size = initial.shape[1]
    blocks = head_major.reshape(seq_rows // MB, MB, 3, head_count, head_size)
    key_rows = blocks[:, :, 1]
    value_rows = blocks[:, :, 2]
    key_gram = jnp.einsum("bmhi,bmhj->bhij", key_rows, key_rows, preferred_element_type=jnp.float32)
    key_value = jnp.einsum(
        "bmhi,bmhj->bhij", key_rows, value_rows, preferred_element_type=jnp.float32
    )
    learn_rate = eta[None, :, None, None]
    identity = jnp.eye(head_size, dtype=jnp.float32)
    linear_all = identity - learn_rate * key_gram
    offset_all = learn_rate * key_value
    start_map = (jnp.broadcast_to(identity, initial.shape), jnp.zeros_like(initial))

    def fold_maps(running, affine):
        return (compose(running, affine), None)

    forward_total, _ = lax.scan(fold_maps, start_map, (linear_all, offset_all))
    backward_total, _ = lax.scan(fold_maps, start_map, (linear_all, offset_all), reverse=True)
    before = prefix(forward_total, "seq", compose, start_map, False)
    after = prefix(backward_total, "seq", compose, start_map, True)
    forward_in = apply_map(before, initial)
    backward_in = apply_map(after, initial)

    def advance(fast_state, affine):
        fresh = apply_map(affine, fast_state)
        return (fresh, fresh)

    _, forward_states = lax.scan(advance, forward_in, (linear_all, offset_all))
    _, backward_states = lax.scan(advance, backward_in, (linear_all, offset_all), reverse=True)
    combined = forward_states + backward_states
    queries = blocks[:, :, 0].astype(jnp.float32)
    read = jnp.einsum("bmhi,bhij->bmhj", queries, combined, precision=precise)
    mean_square = jnp.mean(read * read, axis=-1, keepdims=True)
    normed = (read * lax.rsqrt(mean_square + 1e-06) * gain.reshape(head_count, head_size)).astype(
        jnp.bfloat16
    )
    normed = normed.reshape(seq_rows, head_count * head_size)
    return lax.psum_scatter(
        jnp.dot(normed, w_out, preferred_element_type=jnp.float32),
        "head",
        scatter_dimension=0,
        tiled=True,
    )


def solution(mesh):
    return jax.shard_map(
        shards,
        mesh=mesh,
        in_specs=(
            P(("seq", "head"), None, None),
            P("head"),
            P("head", None, None),
            P("head"),
            P("head", None),
        ),
        out_specs=P(("seq", "head"), None),
        check_vma=False,
    )
```

profile of v0, /device:TPU:1, one launch (start us, length us, event | category | flops | bytes accessed | tf_op | source)
XLA Modules:
  0.0 534.3 jit_solution(7912574881293118915)
XLA Ops:
  6.5 5.8 %copy.17 = bf16[128,3,3072]{0,1,2:T(4,128)(2,1)} copy(bf16[128,3,3072]{2,0,1:T(8,128)(2,1)} %param.17) | data formatting | bytes 4718592 | tf_op args[0]
  12.4 5.8 %all-to-all-start = ((bf16[128,3,3072]{0,1,2:T(4,128)(2,1)}), bf16[128,3,3072]{0,1,2:T(4,128)(2,1)}, u32[]{:S(2)}, u32[]{:S(2)}) async-start(bf16[128,3,3072]{0,1,2:T(4,128)(2,1)} %copy.17), calls=%async_computation | async-start | bytes 6291456 | tf_op jit(solution)/shard_map/all_to_all | solution.py:41
  18.2 37.7 %all-to-all-done = bf16[128,3,3072]{0,1,2:T(4,128)(2,1)} async-done(((bf16[128,3,3072]{0,1,2:T(4,128)(2,1)}), bf16[128,3,3072]{0,1,2:T(4,128)(2,1)}, u32[]{:S(2)}, u32[]{:S(2)}) %all-to-all-start) | async-done | bytes 2359328 | tf_op jit(solution)/shard_map/all_to_all | solution.py:41
  55.9 5.3 copy.33
  61.1 7.0 %reshape.25 = bf16[16,64,3,6,64]{1,0,4,3,2:T(8,128)(2,1)} reshape(bf16[8,128,3,384]{1,0,3,2:T(8,128)(2,1)} %bitcast.146) | data formatting | bytes 4718592 | tf_op jit(solution)/shard_map/reshape | solution.py:45
  68.1 4.8 fusion.52
  73.0 3.0 copy.29
  75.9 3.0 copy.30
  78.9 4.3 convolution_multiply_fusion
  83.2 2.4 multiply_subtract_fusion
  85.7 42.8 %while.92 = (s32[]{:T(128)}, f32[6,64,64]{2,1,0:T(8,128)S(1)}, f32[6,64,64]{2,1,0:T(8,128)S(1)}, f32[16,6,64,64]{3,2,1,0:T(8,128)}, f32[16,6,64,64]{3,2,1,0:T(8,128)}, /*index=5*/s32[]{:T(128)}, s32[]{:T(128)}) while((s32[]{:T(128)}, f32[6,64,64]{2,1,0:T(8,128)S(1)}, f32[6,64,64]{2,1,0:T(8,128)S(1)}, f32[16,6,64,64]{3,2,1,0:T(8,128)}, ...), condition=%wide.region_7.8_spmd, body=%wide.region_6.7_spmd.sunk | while | flops 37773312 | bytes 1377373 | solution.py:62
  130.1 42.9 %while.90 = (s32[]{:T(128)}, f32[6,64,64]{2,1,0:T(8,128)S(1)}, f32[6,64,64]{2,1,0:T(8,128)S(1)}, f32[16,6,64,64]{3,2,1,0:T(8,128)}, f32[16,6,64,64]{3,2,1,0:T(8,128)}, /*index=5*/s32[]{:T(128)}) while((s32[]{:T(128)}, f32[6,64,64]{2,1,0:T(8,128)S(1)}, f32[6,64,64]{2,1,0:T(8,128)S(1)}, f32[16,6,64,64]{3,2,1,0:T(8,128)}, ...), condition=%wide.region_1.2_spmd, body=%wide.region_0.1_spmd.sunk | while | flops 37773312 | bytes 1377361 | solution.py:61
  173.9 3.0 copy.31
  178.0 49.1 %all-gather.13.cloned.1.call-done = f32[96,64,64]{2,1,0:T(8,128)} async-done(((f32[6,64,64]{2,1,0:T(8,128)}), f32[96,64,64]{2,1,0:T(8,128)}) %all-gather.13.cloned.1.call-update) | async-done | bytes 1572880 | tf_op jit(solution)/shard_map/all_gather | solution.py:14
  227.1 43.1 %while.95 = (s32[]{:T(128)}, f32[6,64,64]{2,1,0:T(8,128)S(1)}, f32[6,64,64]{2,1,0:T(8,128)S(1)}, s32[]{:T(128)}, f32[16,6,64,64]{3,2,1,0:T(8,128)}, /*index=5*/f...) while((s32[]{:T(128)}, f32[6,64,64]{2,1,0:T(8,128)S(1)}, ...), condition=%wide.region_9.10_spmd.clone, body=%wide.region_8.9_spmd.clone.sunk | while | flops 37871624 | bytes 1968818 | solution.py:27
  270.3 5.9 %all-gather.11.cloned.1.call-done = f32[96,64,64]{2,1,0:T(8,128)} async-done(((f32[6,64,64]{2,1,0:T(8,128)}), f32[96,64,64]{2,1,0:T(8,128)}) %all-gather.11.cloned.1.call-update) | async-done | bytes 1572880 | tf_op jit(solution)/shard_map/all_gather | solution.py:14
  276.2 48.9 %all-gather.9.cloned.1.call-done = f32[96,64,64]{2,1,0:T(8,128)} async-done(((f32[6,64,64]{2,1,0:T(8,128)}), f32[96,64,64]{2,1,0:T(8,128)}) %all-gather.9.cloned.1.call-update) | async-done | bytes 1572880 | tf_op jit(solution)/shard_map/all_gather | solution.py:14
  325.1 43.0 %while.94 = (s32[]{:T(128)}, f32[6,64,64]{2,1,0:T(8,128)S(1)}, f32[6,64,64]{2,1,0:T(8,128)S(1)}, s32[]{:T(128)}, f32[16,6,64,64]{3,2,1,0:T(8,128)}, /*index=5*/f32[16,6,64,64]{3,2,1,0:T(8,128)}, s32[]{:T(128)}, s32[]{:T(128)}) while((s32[]{:T(128)}, f32[6,64,64]{2,1,0:T(8,128)S(1)}, f32[6,64,64]{2,1,0:T(8,128)S(1)}, s32[]{:T(128)}, ...), condition=%wide.region_3.4_spmd.clone, body=%wide.region_2.3_spmd.clone.sunk | while | flops 37871620 | bytes 1968756 | solution.py:27
  368.5 2.1 broadcast.15.clone
  370.6 32.8 %while.91 = (s32[]{:T(128)}, f32[6,64,64]{2,1,0:T(8,128)S(1)}, f32[16,6,64,64]{3,2,1,0:T(8,128)}, f32[16,6,64,64]{3,2,1,0:T(8,128)}, f32[16,6,64,64]{3,2,1,0:T(8,128)}, /*index=5*/s32[]{:T(128)}) while((s32[]{:T(128)}, f32[6,64,64]{2,1,0:T(8,128)S(1)}, f32[16,6,64,64]{3,2,1,0:T(8,128)}, f32[16,6,64,64]{3,2,1,0:T(8,128)}, ...), condition=%wide.region_5.6_spmd, body=%wide.region_4.5_spmd.sunk | while | flops 18898944 | bytes 984141 | solution.py:72
  385.0 2.0 bitcast_dynamic-update-slice_fusion.4
  387.0 2.1 bitcast_dynamic-update-slice_fusion.4
  389.1 2.0 bitcast_dynamic-update-slice_fusion.4
  403.8 2.1 broadcast.15.clone.1
  405.9 32.8 %while.93 = (s32[]{:T(128)}, f32[6,64,64]{2,1,0:T(8,128)S(1)}, f32[16,6,64,64]{3,2,1,0:T(8,128)}, f32[16,6,64,64]{3,2,1,0:T(8,128)}, f32[16,6,64,64]{3,2,1,0:T(8,128)}, /*index=5*/s32[]{:T(128)}, s32[]{:T(128)}) while((s32[]{:T(128)}, f32[6,64,64]{2,1,0:T(8,128)S(1)}, f32[16,6,64,64]{3,2,1,0:T(8,128)}, f32[16,6,64,64]{3,2,1,0:T(8,128)}, ...), condition=%wide.region_11.12_spmd, body=%wide.region_10.11_spmd.sunk | while | flops 18898948 | bytes 984153 | solution.py:73
  405.9 2.0 bitcast_dynamic-update-slice_fusion.5
  416.1 2.0 bitcast_dynamic-update-slice_fusion.5
  438.6 6.0 %fusion.42 = (f32[16,64,6]{1,2,0:T(8,128)S(1)}, f32[16,6,64,64]{3,2,1,0:T(8,128)S(1)}) fusion(bf16[16,64,1,6,64]{4,1,3,0,2:T(8,128)(2,1)} %copy.31, f32[16,6,64,64]{3,2,1,0:T(8,128)} %get-tuple-element.536, f32[16,6,64,64]{3,2,1,0:T(8,128)} %get-tuple-element.541), kind=kOutput, calls=%fused_computation.54 | convolution fusion | flops 303163392 | bytes 5529600 | tf_op jit(solution)/shard_map/bmhi,bhij->bmhj/dot_general | solution.py:76
  445.4 2.2 copy.25
  447.6 2.7 reshape.26
  450.3 6.4 %fusion.53 = f32[1024,3072]{1,0:T(8,128)} fusion(bf16[1024,384]{0,1:T(8,128)(2,1)S(1)} %reshape.26, bf16[384,3072]{1,0:T(8,128)(2,1)S(1)} %copy-done), kind=kOutput, calls=%fused_computation.72 | convolution fusion | flops 2415919104 | bytes 15728640 | tf_op jit(solution)/shard_map/dot_general | solution.py:83
  456.7 71.0 %reduce-scatter.2.cloned.1.call-done = f32[128,3072]{1,0:T(8,128)} async-done(((f32[1024,3072]{1,0:T(8,128)}), f32[128,3072]{1,0:T(8,128)}) %reduce-scatter.2.cloned.1.call-update) | async-done | bytes 1572880 | tf_op jit(solution)/shard_map/reduce_scatter | solution.py:82
  (358 shorter events, 229.0 us)
Async XLA Ops:
  6.5 443.8 %copy-start = (bf16[384,3072]{1,0:T(8,128)(2,1)S(1)}, bf16[384,3072]{1,0:T(8,128)(2,1)}, u32[]{:S(2)}) copy-start(bf16[384,3072]{1,0:T(8,128)(2,1)} %param.21) | copy-start | bytes 7077892
  12.4 43.5 %all-to-all-start = ((bf16[128,3,3072]{0,1,2:T(4,128)(2,1)}), bf16[128,3,3072]{0,1,2:T(4,128)(2,1)}, u32[]{:S(2)}, u32[]{:S(2)}) async-start(bf16[128,3,3072]{0,1,2:T(4,128)(2,1)} %copy.17), calls=%async_computation | async-start | bytes 6291456 | tf_op jit(solution)/shard_map/all_to_all | solution.py:41
  18.2 159.8 %all-gather.15.cloned.1.call-start = ((), (), s32[]{:S(2)}) async-start(), calls=%async_computation.6 | async-start | bytes 3342336 | tf_op jit(solution)/shard_map/all_gather | solution.py:14
  73.0 5.9 %copy-start.7 = (f32[6]{0:T(128)S(1)}, f32[6]{0:T(128)}, u32[]{:S(2)}) copy-start(f32[6]{0:T(128)} %param.18) | copy-start | bytes 76
  78.9 4.3 copy-start.1
  128.5 0.7 copy-start.3
  128.5 0.7 copy-start.2
  129.2 97.9 %all-gather.13.cloned.1.call-start = ((), (), s32[]{:S(2)}) async-start(), calls=%async_computation.5 | async-start | bytes 3342336 | tf_op jit(solution)/shard_map/all_gather | solution.py:14
  130.0 146.2 %all-gather.11.cloned.1.call-start = ((), (), s32[]{:S(2)}) async-start(), calls=%async_computation.4 | async-start | bytes 3342336 | tf_op jit(solution)/shard_map/all_gather | solution.py:14
  130.1 43.7 %copy-start.8 = (f32[384]{0:T(512)S(1)}, f32[384]{0:T(512)}, u32[]{:S(2)}) copy-start(f32[384]{0:T(512)} %param.20) | copy-start | bytes 4612
  173.0 0.7 copy-start.5
  173.0 3.8 copy-start.4
  173.7 151.4 %all-gather.9.cloned.1.call-start = ((), (), s32[]{:S(2)}) async-start(), calls=%async_computation.3 | async-start | bytes 3342336 | tf_op jit(solution)/shard_map/all_gather | solution.py:14
  176.9 350.9 %reduce-scatter.2.cloned.1.call-start = ((), (), s32[]{:S(2)}) async-start(), calls=%async_computation.2 | async-start | bytes 14155776 | tf_op jit(solution)/shard_map/reduce_scatter | solution.py:82
  325.1 43.0 %copy-start.6 = (f32[6,64,64]{2,1,0:T(8,128)S(1)}, f32[6,64,64]{2,1,0:T(8,128)}, u32[]{:S(2)}) copy-start(f32[6,64,64]{2,1,0:T(8,128)} %param.19) | copy-start | bytes 294916
Sparse Core Ops, SparseCore 0:
  129.3 48.6 all-gather.14
  180.1 46.9 all-gather.12
  229.2 46.9 all-gather.10
  278.2 46.8 all-gather.8
  456.9 70.8 reduce-scatter.1
where the time goes:
time: 538 us; the launch traced here: 534 us
  matrix products  252 us (47%)
  waiting for transfers between devices  214 us (40%)
  local copies, waits for them, and re-layouts  44.7 us (8%)
  between operations  13.4 us (2%)
  starting transfers between devices  6.14 us (1%)
    all_gather x4, waiting for transfers between devices, prefix(): everything = jax.tree.map(lambda part: lax.all_gather(part, axis), value)  105 us
    dot_general x64, matrix products, compose(): jnp.einsum('hij,hjk->hik', later[0], earlier[1], precision=precise)  86.7 us
    dot_general x64, matrix products, compose(): linear = jnp.einsum('hij,hjk->hik', later[0], earlier[0], precision=precise)  80.2 us
    reduce_scatter x1, waiting for transfers between devices, shards(): lax.psum_scatter(jnp.dot(normed, w_out, preferred_element_type=jnp.float3...  71 us
    dot_general x34, matrix products, apply_map(): jnp.einsum('hij,hjk->hik', affine[0], fast_state, precision=precise)  65.7 us
    all_to_all x1, waiting for transfers between devices, shards(): lax.all_to_all(qkv, 'head', split_axis=2, concat_axis=0, tiled=True)  37.7 us
    unnamed x22, local copies, waits for them, and re-layouts  16.1 us
  transfers between devices with their start and end apart: 6, of which 6 were waited for; matrix products, arithmetic and copies ran while one was open for 16% of the time, Pallas kernels for 0%

commit v1 on v0

v1 whole, which is shorter than its diff:
```python
import functools

import jax
import jax.numpy as jnp
from jax import lax
from jax.experimental import pallas as pl
from jax.experimental.pallas import tpu as pltpu
from jax.sharding import PartitionSpec as P

MESH = pl.DeviceIdType.MESH
MB = 64
HD = 64
PAIR = 2 * HD
BF = jnp.bfloat16
F32 = jnp.float32


def split(x):
    high = x.astype(BF)
    return high, (x - high.astype(F32)).astype(BF)


def dot(a, b):
    return lax.dot_general(a, b, (((1,), (0,)), ((), ())), preferred_element_type=F32)


def layer_kernel(
    seqs, heads, pairs,
    qkv, eta, initial, gain, out,
    recv, a_ref, b_ref, pre, totals, inbox, outbox, entry, q_high, q_low, r_ref, normed,
    kv_send, kv_recv, q_send, q_recv, tot_send, tot_recv, fin_send, fin_recv, nrm_send, nrm_recv,
):
    s = lax.axis_index("seq")
    h = lax.axis_index("head")
    x, c = h // 2, h % 2
    xs = heads // 2
    rows = qkv.shape[1]
    width = pairs * PAIR
    subs = rows // MB
    batches = heads * subs
    chains = 4 * pairs

    barrier = pltpu.get_barrier_semaphore()

    def greet_head(d, _):
        pl.semaphore_signal(barrier, inc=1, device_id=(s, (h + d) % heads), device_id_type=MESH)
        return 0

    def greet_seq(d, _):
        pl.semaphore_signal(barrier, inc=1, device_id=((s + d) % seqs, h), device_id_type=MESH)
        return 0

    lax.fori_loop(1, heads, greet_head, 0)
    lax.fori_loop(1, seqs, greet_seq, 0)
    pl.semaphore_wait(barrier, heads + seqs - 2)

    def peer(d, sign):
        dx, dc = d // 2, d % 2
        return ((x + sign * dx + xs) % xs) * 2 + (c + dc) % 2

    def near_first(i):
        step = i // 2
        dx = jnp.where(step < 2, step, xs + 1 - step)
        return dx * 2 + i % 2

    def kv_copy(d):
        to = peer(d, 1)
        return pltpu.make_async_remote_copy(
            src_ref=qkv.at[pl.ds(1, 2), :, pl.ds(pl.multiple_of(to * width, PAIR), width)],
            dst_ref=recv.at[pl.ds(1, 2), pl.ds(pl.multiple_of(h * rows, rows), rows), :],
            send_sem=kv_send.at[d], recv_sem=kv_recv.at[d],
            device_id=(s, to), device_id_type=MESH,
        )

    def q_copy(d):
        to = peer(d, 1)
        return pltpu.make_async_remote_copy(
            src_ref=qkv.at[pl.ds(0, 1), :, pl.ds(pl.multiple_of(to * width, PAIR), width)],
            dst_ref=recv.at[pl.ds(0, 1), pl.ds(pl.multiple_of(h * rows, rows), rows), :],
            send_sem=q_send.at[d], recv_sem=q_recv.at[d],
            device_id=(s, to), device_id_type=MESH,
        )

    def own_copy(first, count, sem):
        return pltpu.make_async_copy(
            qkv.at[pl.ds(first, count), :, pl.ds(pl.multiple_of(h * width, PAIR), width)],
            recv.at[pl.ds(first, count), pl.ds(pl.multiple_of(h * rows, rows), rows), :],
            sem,
        )

    own_copy(1, 2, kv_recv.at[0]).start()

    def start_kv(i, _):
        kv_copy(near_first(heads - i)).start()
        return 0

    def start_q(i, _):
        q_copy(near_first(heads - i)).start()
        return 0

    lax.fori_loop(1, heads, start_kv, 0)
    own_copy(0, 1, q_recv.at[0]).start()
    lax.fori_loop(1, heads, start_q, 0)

    row = lax.broadcasted_iota(jnp.int32, (PAIR, PAIR), 0)
    lane = lax.broadcasted_iota(jnp.int32, (PAIR, PAIR), 1)
    own = (row >= HD) == (lane >= HD)
    eye = jnp.where(row == lane, 1.0, 0.0).astype(F32)

    def grams(i, _):
        d = near_first(i)
        source = peer(d, -1)

        @pl.when(i == 0)
        def _():
            own_copy(1, 2, kv_recv.at[0]).wait()

        @pl.when(i > 0)
        def _():
            kv_copy(d).wait_recv()

        for sub in range(subs):
            at = pl.ds(pl.multiple_of(source * rows + sub * MB, MB), MB)
            b = source * subs + sub
            for p in range(pairs):
                lanes = slice(p * PAIR, (p + 1) * PAIR)
                keys = recv[1, at, lanes]
                values = recv[2, at, lanes]
                swapped = pltpu.roll(values.astype(F32), HD, 1).astype(BF)
                both = lax.dot_general(
                    keys, jnp.concatenate([keys, swapped], axis=1),
                    (((0,), (0,)), ((), ())), preferred_element_type=F32,
                )
                rate = jnp.where(row < HD, eta[2 * p], eta[2 * p + 1])
                high, low = split(jnp.where(own, rate * both[:, :PAIR], 0.0))
                a_ref[b, p, :, :PAIR] = high
                a_ref[b, p, :, PAIR:] = low
                b_ref[b, p] = jnp.where(own, 0.0, rate * both[:, PAIR:])
        return 0

    lax.fori_loop(0, heads, grams, 0)

    for way in range(2):
        b = 0 if way == 0 else batches - 1
        for p in range(pairs):
            a = a_ref[b, p, :, :PAIR].astype(F32) + a_ref[b, p, :, PAIR:].astype(F32)
            pre[way, b, p] = eye - a + b_ref[b, p]

    def advance(t, _):
        for p in range(pairs):
            for way in range(2):
                b = t if way == 0 else batches - 1 - t
                before = b - 1 if way == 0 else b + 1
                state = pre[way, before, p]
                high, low = split(state)
                a = a_ref[b, p]
                change = dot(
                    jnp.concatenate([a, a[:, :PAIR]], axis=1),
                    jnp.concatenate([high, high, low], axis=0),
                )
                pre[way, b, p] = state + b_ref[b, p] - change
        return 0

    lax.fori_loop(1, batches, advance, 0)

    for way in range(2):
        b = batches - 1 if way == 0 else 0
        for p in range(pairs):
            total = pre[way, b, p]
            totals[4 * p + way] = total[:HD]
            totals[4 * p + 2 + way] = total[HD:]

    shift = c * (seqs // 2)
    my_chain = (s + seqs - shift) % seqs
    is_owner = my_chain < chains

    def chain_at(k):
        return (k + shift) % seqs

    def tot_copy(k):
        return pltpu.make_async_remote_copy(
            src_ref=totals.at[k], dst_ref=inbox.at[s],
            send_sem=tot_send.at[k], recv_sem=tot_recv.at[s],
            device_id=(chain_at(k), h), device_id_type=MESH,
        )

    def tot_arrival(source):
        return pltpu.make_async_remote_copy(
            src_ref=totals.at[0], dst_ref=inbox.at[source],
            send_sem=tot_send.at[0], recv_sem=tot_recv.at[source],
            device_id=((s + 1) % seqs, h), device_id_type=MESH,
        )

    def send_total(d, _):
        k = (my_chain + d) % seqs

        @pl.when(k < chains)
        def _():
            tot_copy(k).start()

        return 0

    lax.fori_loop(1, seqs, send_total, 0)

    def fin_copy(k, to):
        return pltpu.make_async_remote_copy(
            src_ref=outbox.at[to], dst_ref=entry.at[k],
            send_sem=fin_send.at[to], recv_sem=fin_recv.at[k],
            device_id=(to, h), device_id_type=MESH,
        )

    def multiply_queries(i):
        source = i // subs
        b = i
        at = pl.ds(pl.multiple_of(b * MB, MB), MB)
        for p in range(pairs):
            query = recv[0, at, p * PAIR:(p + 1) * PAIR]
            ahead, behind = pre[0, b, p], pre[1, b, p]
            high, low = split(jnp.concatenate(
                [jnp.where(own, ahead, 0.0), jnp.where(own, behind, 0.0), jnp.where(own, 0.0, ahead + behind)],
                axis=1,
            ))
            product = dot(jnp.concatenate([query, query], axis=1), jnp.concatenate([high, low], axis=0))
            high, low = split(product[:, :2 * PAIR])
            q_high[p, at, :] = high
            q_low[p, at, :] = low
            r_ref[p, at, :] = product[:, 2 * PAIR:]

    own_copy(0, 1, q_recv.at[0]).wait()

    def wait_q(d, _):
        q_copy(d).wait_recv()
        return 0

    lax.fori_loop(1, heads, wait_q, 0)

    half_lane = lax.broadcasted_iota(jnp.int32, (HD, PAIR), 1)
    half_upper = half_lane >= HD

    @pl.when(is_owner)
    def _():
        inbox[s] = totals[my_chain]
        way = my_chain % 2
        number = my_chain // 2
        odd = number % 2
        mine = half_lane // HD != odd
        start = initial[number]
        state = jnp.where(mine, jnp.concatenate([start, start], axis=1), 0.0)

        def hop(t, state):
            at = jnp.where(way == 0, t, seqs - 1 - t)
            high, low = split(state)
            packed = (high.astype(F32) + pltpu.roll(low.astype(F32), HD, 1)).astype(BF)
            outbox[at] = packed

            @pl.when(at != s)
            def _():
                fin_copy(my_chain, at).start()

            @pl.when(at == s)
            def _():
                entry[my_chain] = packed

            @pl.when(at != s)
            def _():
                tot_arrival(at).wait_recv()

            total = inbox[at]
            linear_high, linear_low = split(jnp.where(mine, 0.0, total))
            change = dot(
                jnp.concatenate([linear_high, linear_low, linear_high], axis=1),
                jnp.concatenate([high, high, high, high, low, low], axis=0),
            )
            multiply_queries(t)
            return jnp.where(mine, total + change, 0.0)

        lax.fori_loop(0, seqs, hop, state)

    @pl.when(jnp.logical_not(is_owner))
    def _():
        def only(t, _):
            multiply_queries(t)
            return 0

        lax.fori_loop(0, batches, only, 0)

    def wait_entry(k, _):
        @pl.when(chain_at(k) != s)
        def _():
            fin_copy(k, (s + 1) % seqs).wait_recv()

        return 0

    lax.fori_loop(0, chains, wait_entry, 0)

    weights = []
    for p in range(pairs):
        highs, lows = [], []
        for way in range(2):
            for odd in range(2):
                packed = entry[4 * p + 2 * odd + way].astype(F32)
                mine = half_upper if odd == 0 else jnp.logical_not(half_upper)
                highs.append(jnp.where(mine, packed, 0.0).astype(BF))
                lows.append(jnp.where(mine, pltpu.roll(packed, HD, 1), 0.0).astype(BF))
        weights.append(jnp.concatenate([jnp.concatenate(highs, axis=0), jnp.concatenate(lows, axis=0)], axis=1))
    mean = jnp.where(own, 1.0 / HD, 0.0).astype(BF)
    mean = jnp.concatenate([mean, mean], axis=0)

    def nrm_copy(d):
        to = peer(d, 1)
        return pltpu.make_async_remote_copy(
            src_ref=normed.at[pl.ds(pl.multiple_of(to * rows, rows), rows), :],
            dst_ref=out.at[:, pl.ds(pl.multiple_of(h * width, PAIR), width)],
            send_sem=nrm_send.at[d], recv_sem=nrm_recv.at[d],
            device_id=(s, to), device_id_type=MESH,
        )

    own_normed = pltpu.make_async_copy(
        normed.at[pl.ds(pl.multiple_of(h * rows, rows), rows), :],
        out.at[:, pl.ds(pl.multiple_of(h * width, PAIR), width)],
        nrm_recv.at[0],
    )

    def read_rows(i, _):
        d = near_first(heads - 1 - i)
        to = peer(d, 1)
        at = pl.ds(pl.multiple_of(to * rows, rows), rows)
        for p in range(pairs):
            product = dot(jnp.concatenate([q_high[p, at, :], q_low[p, at, :]], axis=0), weights[p])
            read = product[:rows, :PAIR] + product[:rows, PAIR:] + product[rows:, :PAIR] + r_ref[p, at, :]
            high, low = split(read * read)
            mean_square = dot(jnp.concatenate([high, low], axis=1), mean)
            value = pltpu.roll(read * lax.rsqrt(mean_square + 1e-06), HD, 1)
            value = value * gain[:, p * PAIR:(p + 1) * PAIR]
            normed[at, p * PAIR:(p + 1) * PAIR] = value.astype(BF)

        @pl.when(i < heads - 1)
        def _():
            nrm_copy(d).start()

        return 0

    lax.fori_loop(0, heads, read_rows, 0)
    own_normed.start()

    def drain_head(d, _):
        nrm_copy(d).wait_recv()
        kv_copy(d).wait_send()
        q_copy(d).wait_send()
        nrm_copy(d).wait_send()
        return 0

    def drain_total(k, _):
        @pl.when(chain_at(k) != s)
        def _():
            tot_copy(k).wait_send()

        return 0

    lax.fori_loop(0, chains, drain_total, 0)

    @pl.when(is_owner)
    def _():
        def drain_fin(to, _):
            @pl.when(to != s)
            def _():
                fin_copy(my_chain, to).wait_send()

            return 0

        lax.fori_loop(0, seqs, drain_fin, 0)

    lax.fori_loop(1, heads, drain_head, 0)
    own_normed.wait()


def layer(qkv, eta, initial, gain, seqs, heads):
    rows = qkv.shape[1]
    width = gain.shape[1]
    pairs = width // PAIR
    tokens = rows * heads
    batches = tokens // MB
    vmem = pl.BlockSpec(memory_space=pltpu.VMEM)
    return pl.pallas_call(
        functools.partial(layer_kernel, seqs, heads, pairs),
        out_shape=jax.ShapeDtypeStruct((rows, heads * width), BF),
        in_specs=[
            pl.BlockSpec(memory_space=pl.ANY), pl.BlockSpec(memory_space=pltpu.SMEM), vmem, vmem,
        ],
        out_specs=vmem,
        scratch_shapes=[
            pltpu.VMEM((3, tokens, width), BF),
            pltpu.VMEM((batches, pairs, PAIR, 2 * PAIR), BF),
            pltpu.VMEM((batches, pairs, PAIR, PAIR), F32),
            pltpu.VMEM((2, batches, pairs, PAIR, PAIR), F32),
            pltpu.VMEM((4 * pairs, HD, PAIR), F32),
            pltpu.VMEM((seqs, HD, PAIR), F32),
            pltpu.VMEM((seqs, HD, PAIR), BF),
            pltpu.VMEM((4 * pairs, HD, PAIR), BF),
            pltpu.VMEM((pairs, tokens, 2 * PAIR), BF),
            pltpu.VMEM((pairs, tokens, 2 * PAIR), BF),
            pltpu.VMEM((pairs, tokens, PAIR), F32),
            pltpu.VMEM((tokens, width), BF),
            pltpu.SemaphoreType.DMA((heads,)), pltpu.SemaphoreType.DMA((heads,)),
            pltpu.SemaphoreType.DMA((heads,)), pltpu.SemaphoreType.DMA((heads,)),
            pltpu.SemaphoreType.DMA((4 * pairs,)), pltpu.SemaphoreType.DMA((seqs,)),
            pltpu.SemaphoreType.DMA((seqs,)), pltpu.SemaphoreType.DMA((4 * pairs,)),
            pltpu.SemaphoreType.DMA((heads,)), pltpu.SemaphoreType.DMA((heads,)),
        ],
        compiler_params=pltpu.CompilerParams(
            collective_id=0, has_side_effects=True, vmem_limit_bytes=40 << 20
        ),
        cost_estimate=pl.CostEstimate(flops=2 << 30, bytes_accessed=200 << 20, transcendentals=0),
    )(qkv, eta, initial, gain)


def solution(mesh):
    seqs, heads = mesh.shape["seq"], mesh.shape["head"]

    def shards(qkv, eta, initial, gain, w_out):
        whole = lax.all_gather(w_out, "head", axis=0, tiled=True)
        normed = layer(jnp.transpose(qkv, (1, 0, 2)), eta, initial, gain[None, :], seqs, heads)
        return jnp.dot(normed, whole, preferred_element_type=F32)

    return jax.shard_map(
        shards,
        mesh=mesh,
        in_specs=(
            P(("seq", "head"), None, None),
            P("head"),
            P("head", None, None),
            P("head"),
            P("head", None),
        ),
        out_specs=P(("seq", "head"), None),
        check_vma=False,
    )
```

time: 538 us -> 152 us (0.28)
  matrix products: 252 us -> 10.1 us
  waiting for transfers between devices: 214 us -> 36.6 us
  Pallas kernels: 0 us -> 87.9 us
  local copies, waits for them, and re-layouts: 44.7 us -> 3.93 us
  starting transfers between devices: 6.14 us -> 0.01 us
    dot_general x166 -> x1, matrix products: 252 us -> 10.1 us  [shards(): return jnp.dot(normed, whole, preferred_element_type=F32)]
    pallas_call x0 -> x1, Pallas kernels: none -> 87.9 us  [layer(): pl.pallas_call(functools.partial(layer_kernel, seqs, heads, pairs), out_s...]
    reduce_scatter x1 -> x0, waiting for transfers between devices: 71 us -> none  [shards(): lax.psum_scatter(jnp.dot(normed, w_out, preferred_element_type=jnp.float3...]
    all_gather x4 -> x1, waiting for transfers between devices: 105 us -> 35.9 us  [shards(): whole = lax.all_gather(w_out, 'head', axis=0, tiled=True)]
    all_to_all x1 -> x0, waiting for transfers between devices: 37.7 us -> none  [shards(): lax.all_to_all(qkv, 'head', split_axis=2, concat_axis=0, tiled=True)]
    unnamed x22 -> x6, local copies, waits for them, and re-layouts: 16.1 us -> 3.25 us
    reshape x2 -> x0, local copies, waits for them, and re-layouts: 9.71 us -> none  [the longest x1 7.01 us: shards(): blocks = head_major.reshape(seq_rows // MB, MB, 3, head_count, head_size)]
    all_to_all x1 -> x0, starting transfers between devices: 5.8 us -> none  [shards(): lax.all_to_all(qkv, 'head', split_axis=2, concat_axis=0, tiled=True)]
  transfers between devices with their start and end apart: 6 -> 1, of which waited for: 6 -> 1; matrix products, arithmetic and copies ran while one was open for 16% -> 0% of each run, Pallas kernels for 0% -> 58%
where the time goes in v1:
time: 152 us
  Pallas kernels  87.9 us (58%)
  waiting for transfers between devices  36.6 us (24%)
  between operations  13.4 us (9%)
  matrix products  10.1 us (7%)
  local copies, waits for them, and re-layouts  3.93 us (3%)
    pallas_call x1, Pallas kernels, layer(): pl.pallas_call(functools.partial(layer_kernel, seqs, heads, pairs), out_s...  87.9 us
    all_gather x1, waiting for transfers between devices, shards(): whole = lax.all_gather(w_out, 'head', axis=0, tiled=True)  35.9 us
    dot_general x1, matrix products, shards(): return jnp.dot(normed, whole, preferred_element_type=F32)  10.1 us
    unnamed x6, local copies, waits for them, and re-layouts  3.25 us
  transfers between devices with their start and end apart: 1, of which 1 were waited for; matrix products, arithmetic and copies ran while one was open for 0% of the time, Pallas kernels for 58%

profile of v1, /device:TPU:1, one launch (start us, length us, event | category | flops | bytes accessed | tf_op | source)
XLA Modules:
  0.0 151.9 jit_solution(3270087706745801831)
XLA Ops:
  6.5 0.0 all-gather.2.cloned.1.call-start
  6.5 0.7 all-gather.2.cloned.1.call-update
  7.3 0.7 broadcast_in_dim.3.gain
  7.9 0.0 copy-start
  7.9 1.7 %copy-done = bf16[128,3,3072]{2,0,1:T(8,128)(2,1)S(1)} copy-done((bf16[128,3,3072]{2,0,1:T(8,128)(2,1)S(1)}, bf16[128,3,3072]{2,0,1:T(8,128)(2,1)}, u32[]{:S(2)}) %copy-start) | copy-done | bytes 2359320
  9.6 0.0 copy-start.1
  9.6 0.9 copy-done.1
  10.5 0.0 copy-start.2
  10.5 0.7 copy-done.2
  11.2 87.9 %shard_map.55 = bf16[128,3072]{1,0:T(8,128)(2,1)S(1)} custom-call(bf16[3,128,3072]{2,1,0:T(8,128)(2,1)S(1)} %bitcast.3, f32[6]{0:T(128)S(1)} %copy-done.2, f32[6,64,64]{2,1,0:T(8,128)S(1)} %copy-done.1, f32[1,384]{1,0:T(1,128)S(1)} %broadcast_in_dim.3.gain), custom_call_target="tpu_custom_call" | custom-call | flops 2147483648 | bytes 209715200 | tf_op jit(solution)/shard_map/pallas_call | solution.py:384
  99.1 35.9 %all-gather.2.cloned.1.call-done = bf16[3072,3072]{1,0:T(8,128)(2,1)} async-done(((bf16[384,3072]{1,0:T(8,128)(2,1)}), bf16[3072,3072]{1,0:T(8,128)(2,1)}) %all-gather.2.cloned.1.call-update) | async-done | bytes 18874384 | tf_op jit(solution)/shard_map/all_gather | solution.py:421
  134.9 10.1 %fusion = f32[128,3072]{1,0:T(8,128)} fusion(bf16[128,3072]{1,0:T(8,128)(2,1)S(1)} %shard_map.55, bf16[3072,3072]{1,0:T(8,128)(2,1)} %all-gather.2.cloned.1.call-done), kind=kOutput, calls=%fused_computation | convolution fusion | flops 2415919104 | bytes 21233664 | tf_op jit(solution)/shard_map/dot_general | solution.py:423
Async XLA Ops:
  6.5 128.4 %all-gather.2.cloned.1.call-start = ((), (), s32[]{:S(2)}) async-start(), calls=%async_computation | async-start | bytes 21233664 | tf_op jit(solution)/shard_map/all_gather | solution.py:421
  7.9 1.7 %copy-start = (bf16[128,3,3072]{2,0,1:T(8,128)(2,1)S(1)}, bf16[128,3,3072]{2,0,1:T(8,128)(2,1)}, u32[]{:S(2)}) copy-start(bf16[128,3,3072]{2,0,1:T(8,128)(2,1)} %param.5) | copy-start | bytes 7077892
  9.6 0.9 copy-start.1
  10.5 0.7 copy-start.2
Sparse Core Ops, SparseCore 0:
  9.0 125.8 all-gather.1

commit v2 on v1

v2 whole, which is shorter than its diff:
```python
import functools

import jax
import jax.numpy as jnp
from jax import lax
from jax.experimental import pallas as pl
from jax.experimental.pallas import tpu as pltpu
from jax.sharding import PartitionSpec as P

MESH = pl.DeviceIdType.MESH
MB = 64
HD = 64
PAIR = 2 * HD
BF = jnp.bfloat16
F32 = jnp.float32


def split(x):
    high = x.astype(BF)
    return high, (x - high.astype(F32)).astype(BF)


def dot(a, b):
    return lax.dot_general(a, b, (((1,), (0,)), ((), ())), preferred_element_type=F32)


def triple(high, low, axis):
    parts = [high, low, high] if axis == 1 else [high, high, low]
    return jnp.concatenate(parts, axis=axis)


def layer_kernel(
    seqs, heads, pairs,
    qkv, eta_hbm, initial_hbm, gain_hbm, w_hbm, out,
    eta, initial, gain, recv, a_ref, b_ref, pre, group, totals, inbox, outbox, entry,
    q_high, q_low, r_ref, normed, normed_in, whole,
    const_sem, own_sem, kv_send, kv_recv, q_send, q_recv, tot_send, tot_recv, fin_send, fin_recv, nrm_send, nrm_recv,
    wx_send, wx_recv, w1_send, w1_recv, w2_send, w2_recv, w3_send, w3_recv, sib_send, sib_recv,
):
    s = lax.axis_index("seq")
    h = lax.axis_index("head")
    x, c = h // 2, h % 2
    xs = heads // 2
    side = 4
    z, y = s // side, s % side
    rows = qkv.shape[1]
    width = pairs * PAIR
    chip_rows = 2 * rows
    group_batches = chip_rows // MB
    chains = 4 * pairs

    barrier = pltpu.get_barrier_semaphore()

    def greet_head(d, _):
        pl.semaphore_signal(barrier, inc=1, device_id=(s, (h + d) % heads), device_id_type=MESH)
        return 0

    def greet_seq(d, _):
        pl.semaphore_signal(barrier, inc=1, device_id=((s + d) % seqs, h), device_id_type=MESH)
        return 0

    lax.fori_loop(1, heads, greet_head, 0)
    lax.fori_loop(1, seqs, greet_seq, 0)

    constants = [
        pltpu.make_async_copy(eta_hbm, eta, const_sem.at[0]),
        pltpu.make_async_copy(initial_hbm, initial, const_sem.at[1]),
        pltpu.make_async_copy(gain_hbm, gain, const_sem.at[2]),
    ]
    for copy in constants:
        copy.start()

    def own_copy(first, count, sem):
        return pltpu.make_async_copy(
            qkv.at[pl.ds(first, count), :, pl.ds(pl.multiple_of(h * width, PAIR), width)],
            recv.at[pl.ds(first, count), pl.ds(pl.multiple_of(h * rows, rows), rows), :],
            sem,
        )

    own_kv = own_copy(1, 2, own_sem.at[0])
    own_q = own_copy(0, 1, own_sem.at[1])
    own_kv.start()
    own_q.start()
    base = c * width
    own_w = pltpu.make_async_copy(w_hbm, whole.at[0, pl.ds(pl.multiple_of(base, PAIR), width), :], own_sem.at[2])
    own_w.start()
    pl.semaphore_wait(barrier, heads + seqs - 2)

    def peer(d, sign):
        dx, dc = d // 2, d % 2
        return ((x + sign * dx + xs) % xs) * 2 + (c + dc) % 2

    half = width // 2
    step = half // side
    cols = w_hbm.shape[1] // side

    def piece(part, first, last, second):
        at = part * half + last * step
        return pl.ds(pl.multiple_of(first + at, 16), step), pl.ds(pl.multiple_of(second * cols, PAIR), cols)

    def wx_copy(part, i):
        last, second = (z, y) if part == 0 else (y, z)
        from_rows, at_cols = piece(part, 0, last, second)
        to_rows, _ = piece(part, base, last, second)
        return pltpu.make_async_remote_copy(
            src_ref=w_hbm.at[from_rows, at_cols],
            dst_ref=whole.at[i, to_rows, at_cols],
            send_sem=wx_send.at[part, i], recv_sem=wx_recv.at[part, i],
            device_id=(s, ((x + xs - i) % xs) * 2 + c), device_id_type=MESH,
        )

    def along(axis, d):
        return (z * side + (y + d) % side, h) if axis == 0 else (((z + d) % side) * side + y, h)

    def w1_copy(part, d):
        last, second = (z, y) if part == 0 else (y, z)
        at_rows, at_cols = piece(part, base, last, second)
        where = whole.at[pl.ds(1, xs - 1), at_rows, at_cols]
        return pltpu.make_async_remote_copy(
            src_ref=where, dst_ref=where,
            send_sem=w1_send.at[part, d], recv_sem=w1_recv.at[part, d],
            device_id=along(part, d), device_id_type=MESH,
        )

    def band(part, d):
        last = z if part == 0 else y
        at_rows, _ = piece(part, base, (last + side - d) % side, 0)
        return whole.at[pl.ds(1, xs - 1), at_rows, :]

    def w2_copy(part, d):
        return pltpu.make_async_remote_copy(
            src_ref=band(part, 0), dst_ref=band(part, 0),
            send_sem=w2_send.at[part, d], recv_sem=w2_recv.at[part, d],
            device_id=along(1 - part, d), device_id_type=MESH,
        )

    def w3_copy(part, d):
        at_cols = pl.ds(0 if d == 1 else 2 * cols, 2 * cols)
        last = z if part == 0 else y
        at_rows, _ = piece(part, base, (last + side - d) % side, 0)
        where = whole.at[pl.ds(1, xs - 1), at_rows, at_cols]
        return pltpu.make_async_remote_copy(
            src_ref=where, dst_ref=where,
            send_sem=w3_send.at[part, d], recv_sem=w3_recv.at[part, d],
            device_id=along(1 - part, d), device_id_type=MESH,
        )

    sibling = (s, x * 2 + 1 - c)

    def sibling_band(part, d):
        return pltpu.make_async_remote_copy(
            src_ref=band(part, d), dst_ref=band(part, d),
            send_sem=sib_send.at[part, d], recv_sem=sib_recv.at[part, d],
            device_id=sibling, device_id_type=MESH,
        )

    sibling_own = pltpu.make_async_remote_copy(
        src_ref=w_hbm, dst_ref=whole.at[0, pl.ds(pl.multiple_of(base, PAIR), width), :],
        send_sem=sib_send.at[2, 0], recv_sem=sib_recv.at[2, 0],
        device_id=sibling, device_id_type=MESH,
    )

    def kv_copy(d):
        to = peer(d, 1)
        return pltpu.make_async_remote_copy(
            src_ref=qkv.at[pl.ds(1, 2), :, pl.ds(pl.multiple_of(to * width, PAIR), width)],
            dst_ref=recv.at[pl.ds(1, 2), pl.ds(pl.multiple_of(h * rows, rows), rows), :],
            send_sem=kv_send.at[d], recv_sem=kv_recv.at[d],
            device_id=(s, to), device_id_type=MESH,
        )

    def q_copy(d):
        to = peer(d, 1)
        return pltpu.make_async_remote_copy(
            src_ref=qkv.at[pl.ds(0, 1), :, pl.ds(pl.multiple_of(to * width, PAIR), width)],
            dst_ref=recv.at[pl.ds(0, 1), pl.ds(pl.multiple_of(h * rows, rows), rows), :],
            send_sem=q_send.at[d], recv_sem=q_recv.at[d],
            device_id=(s, to), device_id_type=MESH,
        )

    def loop(first, last, act):
        def run(i, _):
            act(i)
            return 0

        lax.fori_loop(first, last, run, 0)

    hops = [0, 1, 3, 2]

    kv_copy(1).start()
    for part in range(2):
        for i in hops[1:]:
            wx_copy(part, i).start()
    for dx in (2, 1, 3):
        kv_copy(2 * dx).start()
        kv_copy(2 * dx + 1).start()
    q_copy(1).start()
    for dx in (2, 1, 3):
        q_copy(2 * dx).start()
        q_copy(2 * dx + 1).start()
    sibling_own.start()

    row = lax.broadcasted_iota(jnp.int32, (PAIR, PAIR), 0)
    lane = lax.broadcasted_iota(jnp.int32, (PAIR, PAIR), 1)
    own = (row >= HD) == (lane >= HD)
    eye = jnp.where(row == lane, 1.0, 0.0).astype(F32)

    for copy in constants:
        copy.wait()

    def chip_maps(dx):
        at_x = (x + xs - dx) % xs

        def grams(i):
            at = pl.ds(pl.multiple_of(at_x * chip_rows + i * MB, MB), MB)
            for p in range(pairs):
                lanes = slice(p * PAIR, (p + 1) * PAIR)
                keys = recv[1, at, lanes]
                values = recv[2, at, lanes]
                swapped = pltpu.roll(values.astype(F32), HD, 1).astype(BF)
                both = lax.dot_general(
                    keys, jnp.concatenate([keys, swapped], axis=1),
                    (((0,), (0,)), ((), ())), preferred_element_type=F32,
                )
                rate = jnp.where(row < HD, eta[2 * p], eta[2 * p + 1])
                linear = jnp.where(own, rate * both[:, :PAIR], 0.0)
                offset = jnp.where(own, 0.0, rate * both[:, PAIR:])
                high, low = split(linear)
                a_ref[i, p, :, :PAIR] = high
                a_ref[i, p, :, PAIR:] = low
                b_ref[i, p] = offset
                first = eye - linear + offset

                @pl.when(i == 0)
                def _():
                    pre[0, at_x * group_batches, p] = first

                @pl.when(i == group_batches - 1)
                def _():
                    pre[1, at_x * group_batches + i, p] = first

        loop(0, group_batches, grams)

        def advance(t):
            for p in range(pairs):
                for way in range(2):
                    i = t if way == 0 else group_batches - 1 - t
                    before = i - 1 if way == 0 else i + 1
                    state = pre[way, at_x * group_batches + before, p]
                    high, low = split(state)
                    a = a_ref[i, p]
                    change = dot(jnp.concatenate([a, a[:, :PAIR]], axis=1), triple(high, low, 0))
                    pre[way, at_x * group_batches + i, p] = state + b_ref[i, p] - change

        loop(1, group_batches, advance)

    own_kv.wait()
    kv_copy(1).wait_recv()
    chip_maps(0)

    for part in range(2):
        for i in hops[1:]:
            wx_copy(part, i).wait_recv()
    for part in range(2):
        for d in (2, 1, 3):
            w1_copy(part, d).start()

    for dx in (1, 3):
        kv_copy(2 * dx).wait_recv()
        kv_copy(2 * dx + 1).wait_recv()
        chip_maps(dx)

    for part in range(2):
        for d in (1, 2, 3):
            w1_copy(part, d).wait_recv()
    for part in range(2):
        for d in (1, 3):
            w2_copy(part, d).start()
    for part in range(2):
        sibling_band(part, 0).start()

    kv_copy(4).wait_recv()
    kv_copy(5).wait_recv()
    chip_maps(2)

    def linear_of(total):
        return triple(*split(jnp.where(own, total, 0.0)), 1)

    for p in range(pairs):
        group[0, 0, p] = pre[0, group_batches - 1, p]
        group[1, xs - 1, p] = pre[1, (xs - 1) * group_batches, p]

    def advance_chip(t):
        for p in range(pairs):
            for way in range(2):
                g = t if way == 0 else xs - 1 - t
                before = g - 1 if way == 0 else g + 1
                b = (g + 1) * group_batches - 1 if way == 0 else g * group_batches
                total = pre[way, b, p]
                change = dot(linear_of(total), triple(*split(group[way, before, p]), 0))
                group[way, g, p] = jnp.where(own, 0.0, total) + change

    loop(1, xs, advance_chip)

    for way in range(2):
        for p in range(pairs):
            total = group[way, xs - 1 if way == 0 else 0, p]
            totals[4 * p + way] = total[:HD]
            totals[4 * p + 2 + way] = total[HD:]

    shift = c * (seqs // 2)
    my_chain = (s + seqs - shift) % seqs
    is_owner = my_chain < chains

    def chain_at(k):
        return (k + shift) % seqs

    def tot_copy(k):
        return pltpu.make_async_remote_copy(
            src_ref=totals.at[k], dst_ref=inbox.at[s],
            send_sem=tot_send.at[k], recv_sem=tot_recv.at[s],
            device_id=(chain_at(k), h), device_id_type=MESH,
        )

    def tot_arrival(source):
        return pltpu.make_async_remote_copy(
            src_ref=totals.at[0], dst_ref=inbox.at[source],
            send_sem=tot_send.at[0], recv_sem=tot_recv.at[source],
            device_id=((s + 1) % seqs, h), device_id_type=MESH,
        )

    def send_total(d):
        k = (my_chain + d) % seqs

        @pl.when(k < chains)
        def _():
            tot_copy(k).start()

    loop(1, seqs, send_total)

    def fin_copy(k, to):
        return pltpu.make_async_remote_copy(
            src_ref=outbox.at[to], dst_ref=entry.at[k],
            send_sem=fin_send.at[to], recv_sem=fin_recv.at[k],
            device_id=(to, h), device_id_type=MESH,
        )

    def multiply_queries(dx):
        at_x = (x + xs - dx) % xs

        def one(i):
            b = at_x * group_batches + i
            at = pl.ds(pl.multiple_of(b * MB, MB), MB)
            for p in range(pairs):
                query = recv[0, at, p * PAIR:(p + 1) * PAIR]
                ahead, behind = pre[0, b, p], pre[1, b, p]
                high, low = split(jnp.concatenate(
                    [jnp.where(own, ahead, 0.0), jnp.where(own, behind, 0.0), jnp.where(own, 0.0, ahead + behind)],
                    axis=1,
                ))
                product = dot(jnp.concatenate([query, query], axis=1), jnp.concatenate([high, low], axis=0))
                high, low = split(product[:, :2 * PAIR])
                q_high[p, at, :] = high
                q_low[p, at, :] = low
                r_ref[p, at, :] = product[:, 2 * PAIR:]

        loop(0, group_batches, one)

    own_q.wait()
    q_copy(1).wait_recv()
    multiply_queries(0)
    for dx in (1, 3):
        q_copy(2 * dx).wait_recv()
        q_copy(2 * dx + 1).wait_recv()
        multiply_queries(dx)

    @pl.when(is_owner)
    def _():
        inbox[s] = totals[my_chain]
        way = my_chain % 2
        number = my_chain // 2
        odd = number % 2
        half_lane = lax.broadcasted_iota(jnp.int32, (HD, PAIR), 1)
        mine = half_lane // HD != odd
        start = initial[number]

        def place(t):
            return jnp.where(way == 0, t, seqs - 1 - t)

        def arrive(source):
            @pl.when(source != s)
            def _():
                tot_arrival(source).wait_recv()

        loop(0, seqs, arrive)

        def apply(total, high, low):
            linear_high, linear_low = split(jnp.where(mine, 0.0, total))
            return jnp.where(mine, total, 0.0) + dot(
                triple(linear_high, linear_low, 1),
                jnp.concatenate([high, high, high, high, low, low], axis=0),
            )

        def emit(t, state):
            at = place(t)
            high, low = split(state)
            packed = (high.astype(F32) + pltpu.roll(low.astype(F32), HD, 1)).astype(BF)
            outbox[at] = packed

            @pl.when(at != s)
            def _():
                fin_copy(my_chain, at).start()

            @pl.when(at == s)
            def _():
                entry[my_chain] = packed

        quads = seqs // side
        maps = [[None] * side for _ in range(quads)]
        for j in range(side):
            for g in range(quads):
                total = inbox[place(g * side + j)]
                maps[g][j] = total if j == 0 else apply(total, *split(maps[g][j - 1]))
        state = jnp.where(mine, jnp.concatenate([start, start], axis=1), 0.0)
        states = [state]
        for g in range(quads - 1):
            states.append(jnp.where(mine, apply(maps[g][side - 1], *split(states[-1])), 0.0))
        for g in range(quads):
            emit(g * side, states[g])
            parts = split(states[g])
            for j in range(side - 1):
                emit(g * side + j + 1, jnp.where(mine, apply(maps[g][j], *parts), 0.0))

    q_copy(4).wait_recv()
    q_copy(5).wait_recv()
    multiply_queries(2)

    def wait_entry(k):
        @pl.when(chain_at(k) != s)
        def _():
            fin_copy(k, (s + 1) % seqs).wait_recv()

    loop(0, chains, wait_entry)

    half_upper = lax.broadcasted_iota(jnp.int32, (HD, PAIR), 1) >= HD
    mean = jnp.where(own, 1.0 / HD, 0.0).astype(BF)
    mean = jnp.concatenate([mean, mean], axis=0)
    entered = []
    for p in range(pairs):
        ways = []
        for way in range(2):
            highs, lows = [], []
            for odd in range(2):
                packed = entry[4 * p + 2 * odd + way].astype(F32)
                mine = half_upper if odd == 0 else jnp.logical_not(half_upper)
                highs.append(jnp.where(mine, packed, 0.0).astype(BF))
                lows.append(jnp.where(mine, pltpu.roll(packed, HD, 1), 0.0).astype(BF))
            ways.append((jnp.concatenate(highs, axis=0), jnp.concatenate(lows, axis=0)))
        entered.append(ways)

    def nrm_copy(d):
        to = peer(d, 1)
        return pltpu.make_async_remote_copy(
            src_ref=normed.at[pl.ds(pl.multiple_of(to * rows, rows), rows), :],
            dst_ref=normed_in.at[(xs - d // 2) % xs, :, pl.ds(pl.multiple_of(c * width, PAIR), width)],
            send_sem=nrm_send.at[d], recv_sem=nrm_recv.at[d],
            device_id=(s, to), device_id_type=MESH,
        )

    own_normed = pltpu.make_async_copy(
        normed.at[pl.ds(pl.multiple_of(h * rows, rows), rows), :],
        normed_in.at[0, :, pl.ds(pl.multiple_of(c * width, PAIR), width)],
        own_sem.at[3],
    )

    def read_chip(dx):
        at_x = (x + dx) % xs
        at = pl.ds(pl.multiple_of(at_x * chip_rows, chip_rows), chip_rows)
        for p in range(pairs):
            highs, lows = [], []
            for way in range(2):
                high, low = entered[p][way]
                before = (at_x + xs - 1) % xs if way == 0 else (at_x + 1) % xs
                total = group[way, before, p]
                moved = jnp.where(own, 0.0, total) + dot(linear_of(total), triple(high, low, 0))
                edge = at_x == (0 if way == 0 else xs - 1)
                moved_high, moved_low = split(jnp.where(own, 0.0, moved))
                highs.append(jnp.where(edge, high, moved_high))
                lows.append(jnp.where(edge, low, moved_low))
            weight = jnp.concatenate([jnp.concatenate(highs, axis=0), jnp.concatenate(lows, axis=0)], axis=1)
            product = dot(q_high[p, at, :], weight)
            read = product[:, :PAIR] + product[:, PAIR:] + dot(q_low[p, at, :], weight[:, :PAIR]) + r_ref[p, at, :]
            high, low = split(read * read)
            mean_square = dot(jnp.concatenate([high, low], axis=1), mean)
            value = pltpu.roll(read * lax.rsqrt(mean_square + 1e-06), HD, 1)
            value = value * gain[:, p * PAIR:(p + 1) * PAIR]
            normed[at, p * PAIR:(p + 1) * PAIR] = value.astype(BF)

    for dx in (2, 1, 3, 0):
        read_chip(dx)
        if dx:
            nrm_copy(2 * dx).start()
        else:
            own_normed.start()
        nrm_copy(2 * dx + 1).start()

    for part in range(2):
        for d in (1, 3):
            w2_copy(part, d).wait_recv()
            w3_copy(part, d).start()
            sibling_band(part, d).start()
    for part in range(2):
        for d in (1, 3):
            w3_copy(part, d).wait_recv()
        sibling_band(part, 2).start()

    own_w.wait()
    sibling_own.wait_recv()
    own_normed.wait()
    for d in range(1, heads):
        nrm_copy(d).wait_recv()

    def sibling_arrival(part, d):
        last = z if part == 0 else y
        at_rows, _ = piece(part, width - base, (last + side - d) % side, 0)
        where = whole.at[pl.ds(1, xs - 1), at_rows, :]
        return pltpu.make_async_remote_copy(
            src_ref=where, dst_ref=where,
            send_sem=sib_send.at[part, d], recv_sem=sib_recv.at[part, d],
            device_id=sibling, device_id_type=MESH,
        )

    for part in range(2):
        for d in range(side):
            sibling_arrival(part, d).wait_recv()

    tile = 512

    def project(j):
        at = pl.ds(pl.multiple_of(j * tile, tile), tile)
        total = dot(normed_in[0], whole[0, :, at])
        for i in range(1, xs):
            total = total + dot(normed_in[i], whole[i, :, at])
        out[:, at] = total

    loop(0, w_hbm.shape[1] // tile, project)

    for part in range(2):
        for i in range(1, xs):
            wx_copy(part, i).wait_send()
            w1_copy(part, i).wait_send()
        for d in (1, 3):
            w2_copy(part, d).wait_send()
            w3_copy(part, d).wait_send()
        for d in range(side):
            sibling_band(part, d).wait_send()
    sibling_own.wait_send()

    def drain_head(d):
        kv_copy(d).wait_send()
        q_copy(d).wait_send()
        nrm_copy(d).wait_send()

    def drain_total(k):
        @pl.when(chain_at(k) != s)
        def _():
            tot_copy(k).wait_send()

    loop(1, heads, drain_head)
    loop(0, chains, drain_total)

    @pl.when(is_owner)
    def _():
        def drain_fin(to):
            @pl.when(to != s)
            def _():
                fin_copy(my_chain, to).wait_send()

        loop(0, seqs, drain_fin)


def layer(qkv, eta, initial, gain, w_out, seqs, heads):
    rows = qkv.shape[1]
    width, columns = w_out.shape
    pairs = width // PAIR
    tokens = rows * heads
    batches = tokens // MB
    xs = heads // 2
    anywhere = pl.BlockSpec(memory_space=pl.ANY)
    dma = pltpu.SemaphoreType.DMA
    return pl.pallas_call(
        functools.partial(layer_kernel, seqs, heads, pairs),
        out_shape=jax.ShapeDtypeStruct((rows, columns), F32),
        in_specs=[anywhere] * 5,
        out_specs=pl.BlockSpec(memory_space=pltpu.VMEM),
        scratch_shapes=[
            pltpu.SMEM(eta.shape, F32),
            pltpu.VMEM(initial.shape, F32),
            pltpu.VMEM(gain.shape, F32),
            pltpu.VMEM((3, tokens, width), BF),
            pltpu.VMEM((batches // xs, pairs, PAIR, 2 * PAIR), BF),
            pltpu.VMEM((batches // xs, pairs, PAIR, PAIR), F32),
            pltpu.VMEM((2, batches, pairs, PAIR, PAIR), F32),
            pltpu.VMEM((2, xs, pairs, PAIR, PAIR), F32),
            pltpu.VMEM((4 * pairs, HD, PAIR), F32),
            pltpu.VMEM((seqs, HD, PAIR), F32),
            pltpu.VMEM((seqs, HD, PAIR), BF),
            pltpu.VMEM((4 * pairs, HD, PAIR), BF),
            pltpu.VMEM((pairs, tokens, 2 * PAIR), BF),
            pltpu.VMEM((pairs, tokens, 2 * PAIR), BF),
            pltpu.VMEM((pairs, tokens, PAIR), F32),
            pltpu.VMEM((tokens, width), BF),
            pltpu.VMEM((xs, rows, 2 * width), BF),
            pltpu.VMEM((xs, 2 * width, columns), BF),
            dma((3,)), dma((4,)),
            dma((heads,)), dma((heads,)), dma((heads,)), dma((heads,)),
            dma((4 * pairs,)), dma((seqs,)), dma((seqs,)), dma((4 * pairs,)),
            dma((heads,)), dma((heads,)),
            dma((2, 4)), dma((2, 4)), dma((2, 4)), dma((2, 4)), dma((2, 4)), dma((2, 4)),
            dma((2, 4)), dma((2, 4)), dma((3, 4)), dma((3, 4)),
        ],
        compiler_params=pltpu.CompilerParams(
            collective_id=0, has_side_effects=True, vmem_limit_bytes=57 << 20
        ),
    )(qkv, eta, initial, gain, w_out)


def solution(mesh):
    seqs, heads = mesh.shape["seq"], mesh.shape["head"]

    def shards(qkv, eta, initial, gain, w_out):
        return layer(jnp.transpose(qkv, (1, 0, 2)), eta, initial, gain[None, :], w_out, seqs, heads)

    return jax.shard_map(
        shards,
        mesh=mesh,
        in_specs=(
            P(("seq", "head"), None, None),
            P("head"),
            P("head", None, None),
            P("head"),
            P("head", None),
        ),
        out_specs=P(("seq", "head"), None),
        check_vma=False,
    )
```

time: 152 us -> 110 us (0.72)
  the two profiles are of different devices: /device:TPU:1 before, /device:TPU:3 now
where the time goes in v2:
time: 110 us
  Pallas kernels  106 us (96%)
  local copies, waits for them, and re-layouts  3.95 us (4%)
    pallas_call x1, Pallas kernels, layer(): pl.pallas_call(functools.partial(layer_kernel, seqs, heads, pairs), out_s...  106 us
    unnamed x1, local copies, waits for them, and re-layouts  2.7 us

profile of v2, /device:TPU:3, one launch (start us, length us, event | category | flops | bytes accessed | tf_op | source)
XLA Modules:
  0.0 110.2 jit_solution(12867204939473460572)
XLA Ops:
  0.0 1.2 %broadcast_in_dim.3.gain_hbm = f32[1,384]{1,0:T(1,128)} reshape(f32[384]{0:T(512)} %param.8) | data formatting | bytes 3072 | tf_op jit(solution)/shard_map/broadcast_in_dim | solution.py:632
  1.2 106.2 %shard_map.55 = f32[128,3072]{1,0:T(8,128)} custom-call(bf16[3,128,3072]{2,1,0:T(8,128)(2,1)} %bitcast.1, f32[6]{0:T(128)} %eta_hbm.1, f32[6,64,64]{2,1,0:T(8,128)} %initial_hbm.1, f32[1,384]{1,0:T(1,128)} %broadcast_in_dim.3.gain_hbm, bf16[384,3072]{1,0:T(8,128)(2,1)} %w_hbm.1), custom_call_target="tpu_custom_call" | custom-call | tf_op jit(solution)/shard_map/pallas_call | solution.py:591
  107.5 2.7 %copy.7 = f32[128,3072]{1,0:T(8,128)} copy(f32[128,3072]{1,0:T(8,128)} %shard_map.55) | data formatting | bytes 3145728

commit v3 on v2

--- a/solution.py
+++ b/solution.py
@@ -185,20 +185,16 @@
 
         lax.fori_loop(first, last, run, 0)
 
-    hops = [0, 1, 3, 2]
-
     kv_copy(1).start()
     for part in range(2):
-        for i in hops[1:]:
+        for i in (1, 3, 2):
             wx_copy(part, i).start()
-    for dx in (2, 1, 3):
-        kv_copy(2 * dx).start()
-        kv_copy(2 * dx + 1).start()
+    for d in (2, 3, 6, 7):
+        kv_copy(d).start()
     q_copy(1).start()
-    for dx in (2, 1, 3):
-        q_copy(2 * dx).start()
-        q_copy(2 * dx + 1).start()
-    sibling_own.start()
+
+    def near(i):
+        return jnp.where(i < 2, i, xs + 1 - i)
 
     row = lax.broadcasted_iota(jnp.int32, (PAIR, PAIR), 0)
     lane = lax.broadcasted_iota(jnp.int32, (PAIR, PAIR), 1)
@@ -208,10 +204,26 @@
     for copy in constants:
         copy.wait()
 
-    def chip_maps(dx):
+    own_kv.wait()
+    rates = [jnp.where(row < HD, eta[2 * p], eta[2 * p + 1]) for p in range(pairs)]
+
+    def chip_maps(n):
+        dx = near(n)
         at_x = (x + xs - dx) % xs
 
-        def grams(i):
+        @pl.when(n > 0)
+        def _():
+            kv_copy(2 * dx).wait_recv()
+
+        kv_copy(2 * dx + 1).wait_recv()
+
+        @pl.when(n == xs - 1)
+        def _():
+            for d in range(2, heads):
+                q_copy(d).start()
+
+        first = {}
+        for i in range(group_batches):
             at = pl.ds(pl.multiple_of(at_x * chip_rows + i * MB, MB), MB)
             for p in range(pairs):
                 lanes = slice(p * PAIR, (p + 1) * PAIR)
@@ -222,91 +234,79 @@
                     keys, jnp.concatenate([keys, swapped], axis=1),
                     (((0,), (0,)), ((), ())), preferred_element_type=F32,
                 )
-                rate = jnp.where(row < HD, eta[2 * p], eta[2 * p + 1])
-                linear = jnp.where(own, rate * both[:, :PAIR], 0.0)
-                offset = jnp.where(own, 0.0, rate * both[:, PAIR:])
+                linear = jnp.where(own, rates[p] * both[:, :PAIR], 0.0)
+                offset = jnp.where(own, 0.0, rates[p] * both[:, PAIR:])
                 high, low = split(linear)
                 a_ref[i, p, :, :PAIR] = high
                 a_ref[i, p, :, PAIR:] = low
                 b_ref[i, p] = offset
-                first = eye - linear + offset
-
-                @pl.when(i == 0)
-                def _():
-                    pre[0, at_x * group_batches, p] = first
-
-                @pl.when(i == group_batches - 1)
-                def _():
-                    pre[1, at_x * group_batches + i, p] = first
-
-        loop(0, group_batches, grams)
-
-        def advance(t):
+                if i in (0, group_batches - 1):
+                    first[i, p] = eye - linear + offset
+        base_batch = at_x * group_batches
+        states = {}
+        for p in range(pairs):
+            for way in range(2):
+                i = 0 if way == 0 else group_batches - 1
+                states[way, p] = first[i, p]
+                pre[way, base_batch + i, p] = first[i, p]
+        for t in range(1, group_batches):
             for p in range(pairs):
                 for way in range(2):
                     i = t if way == 0 else group_batches - 1 - t
-                    before = i - 1 if way == 0 else i + 1
-                    state = pre[way, at_x * group_batches + before, p]
+                    state = states[way, p]
                     high, low = split(state)
                     a = a_ref[i, p]
                     change = dot(jnp.concatenate([a, a[:, :PAIR]], axis=1), triple(high, low, 0))
-                    pre[way, at_x * group_batches + i, p] = state + b_ref[i, p] - change
-
-        loop(1, group_batches, advance)
-
-    own_kv.wait()
-    kv_copy(1).wait_recv()
-    chip_maps(0)
-
-    for part in range(2):
-        for i in hops[1:]:
-            wx_copy(part, i).wait_recv()
-    for part in range(2):
-        for d in (2, 1, 3):
-            w1_copy(part, d).start()
-
-    for dx in (1, 3):
-        kv_copy(2 * dx).wait_recv()
-        kv_copy(2 * dx + 1).wait_recv()
-        chip_maps(dx)
-
-    for part in range(2):
-        for d in (1, 2, 3):
-            w1_copy(part, d).wait_recv()
-    for part in range(2):
-        for d in (1, 3):
-            w2_copy(part, d).start()
-    for part in range(2):
-        sibling_band(part, 0).start()
-
-    kv_copy(4).wait_recv()
-    kv_copy(5).wait_recv()
-    chip_maps(2)
+                    states[way, p] = state + b_ref[i, p] - change
+                    pre[way, base_batch + i, p] = states[way, p]
+
+        @pl.when(n == 0)
+        def _():
+            sibling_own.start()
+            for part in range(2):
+                for i in range(1, xs):
+                    wx_copy(part, i).wait_send()
+            for d in (4, 5):
+                kv_copy(d).start()
+            for part in range(2):
+                for i in range(1, xs):
+                    wx_copy(part, i).wait_recv()
+            for part in range(2):
+                for d in (2, 1, 3):
+                    w1_copy(part, d).start()
+
+        @pl.when(n == 2)
+        def _():
+            for part in range(2):
+                for d in (1, 2, 3):
+                    w1_copy(part, d).wait_recv()
+            for part in range(2):
+                for d in (1, 3):
+                    w2_copy(part, d).start()
+            for part in range(2):
+                sibling_band(part, 0).start()
+
+    loop(0, xs, chip_maps)
 
     def linear_of(total):
         return triple(*split(jnp.where(own, total, 0.0)), 1)
 
-    for p in range(pairs):
-        group[0, 0, p] = pre[0, group_batches - 1, p]
-        group[1, xs - 1, p] = pre[1, (xs - 1) * group_batches, p]
-
-    def advance_chip(t):
+    states = {}
+    for t in range(xs):
         for p in range(pairs):
             for way in range(2):
                 g = t if way == 0 else xs - 1 - t
-                before = g - 1 if way == 0 else g + 1
                 b = (g + 1) * group_batches - 1 if way == 0 else g * group_batches
                 total = pre[way, b, p]
-                change = dot(linear_of(total), triple(*split(group[way, before, p]), 0))
-                group[way, g, p] = jnp.where(own, 0.0, total) + change
-
-    loop(1, xs, advance_chip)
-
+                if t:
+                    change = dot(linear_of(total), triple(*split(states[way, p]), 0))
+                    total = jnp.where(own, 0.0, total) + change
+                states[way, p] = total
+                group[way, g, p] = total
     for way in range(2):
         for p in range(pairs):
-            total = group[way, xs - 1 if way == 0 else 0, p]
-            totals[4 * p + way] = total[:HD]
-            totals[4 * p + 2 + way] = total[HD:]
+            totals[4 * p + way] = states[way, p][:HD]
+            totals[4 * p + 2 + way] = states[way, p][HD:]
 
     shift = c * (seqs // 2)
     my_chain = (s + seqs - shift) % seqs
@@ -347,6 +347,12 @@
 
     def multiply_queries(dx):
         at_x = (x + xs - dx) % xs
+
+        @pl.when(dx > 0)
+        def _():
+            q_copy(2 * dx).wait_recv()
+
+        q_copy(2 * dx + 1).wait_recv()
 
         def one(i):
             b = at_x * group_batches + i
@@ -367,12 +373,7 @@
         loop(0, group_batches, one)
 
     own_q.wait()
-    q_copy(1).wait_recv()
-    multiply_queries(0)
-    for dx in (1, 3):
-        q_copy(2 * dx).wait_recv()
-        q_copy(2 * dx + 1).wait_recv()
-        multiply_queries(dx)
+    loop(0, xs - 1, lambda n: multiply_queries(near(n)))
 
     @pl.when(is_owner)
     def _():
@@ -402,18 +403,8 @@
             )
 
         def emit(t, state):
-            at = place(t)
             high, low = split(state)
-            packed = (high.astype(F32) + pltpu.roll(low.astype(F32), HD, 1)).astype(BF)
-            outbox[at] = packed
-
-            @pl.when(at != s)
-            def _():
-                fin_copy(my_chain, at).start()
-
-            @pl.when(at == s)
-            def _():
-                entry[my_chain] = packed
+            outbox[place(t)] = (high.astype(F32) + pltpu.roll(low.astype(F32), HD, 1)).astype(BF)
 
         quads = seqs // side
         maps = [[None] * side for _ in range(quads)]
@@ -431,9 +422,10 @@
             for j in range(side - 1):
                 emit(g * side + j + 1, jnp.where(mine, apply(maps[g][j], *parts), 0.0))
 
-    q_copy(4).wait_recv()
-    q_copy(5).wait_recv()
-    multiply_queries(2)
+        entry[my_chain] = outbox[s]
+        loop(1, seqs, lambda d: fin_copy(my_chain, (s + d) % seqs).start())
+
+    multiply_queries(jnp.int32(xs // 2))
 
     def wait_entry(k):
         @pl.when(chain_at(k) != s)
@@ -493,16 +485,21 @@
             high, low = split(read * read)
             mean_square = dot(jnp.concatenate([high, low], axis=1), mean)
             value = pltpu.roll(read * lax.rsqrt(mean_square + 1e-06), HD, 1)
-            value = value * gain[:, p * PAIR:(p + 1) * PAIR]
+            value = value * gain[p * PAIR:(p + 1) * PAIR]
             normed[at, p * PAIR:(p + 1) * PAIR] = value.astype(BF)
 
-    for dx in (2, 1, 3, 0):
+    def read_and_send(n):
+        dx = near(xs - 1 - n)
         read_chip(dx)
-        if dx:
+
+        @pl.when(dx > 0)
+        def _():
             nrm_copy(2 * dx).start()
-        else:
-            own_normed.start()
+
         nrm_copy(2 * dx + 1).start()
+
+    loop(0, xs, read_and_send)
+    own_normed.start()
 
     for part in range(2):
         for d in (1, 3):
@@ -547,7 +544,6 @@
 
     for part in range(2):
         for i in range(1, xs):
-            wx_copy(part, i).wait_send()
             w1_copy(part, i).wait_send()
         for d in (1, 3):
             w2_copy(part, d).wait_send()
@@ -629,7 +625,7 @@
     seqs, heads = mesh.shape["seq"], mesh.shape["head"]
 
     def shards(qkv, eta, initial, gain, w_out):
-        return layer(jnp.transpose(qkv, (1, 0, 2)), eta, initial, gain[None, :], w_out, seqs, heads)
+        return layer(jnp.transpose(qkv, (1, 0, 2)), eta, initial, gain, w_out, seqs, heads)
 
     return jax.shard_map(
         shards,

time: 110 us -> 93.6 us (0.85)
  the two profiles are of different devices: /device:TPU:3 before, /device:TPU:1 now
where the time goes in v3:
time: 93.6 us; the launch traced here: 93.5 us
  Pallas kernels  90.8 us (97%)
  local copies, waits for them, and re-layouts  2.7 us (3%)
    pallas_call x1, Pallas kernels, layer(): pl.pallas_call(functools.partial(layer_kernel, seqs, heads, pairs), out_s...  90.8 us
    unnamed x1, local copies, waits for them, and re-layouts  2.7 us

profile of v3, /device:TPU:1, one launch (start us, length us, event | category | flops | bytes accessed | tf_op | source)
XLA Modules:
  0.0 93.5 jit_solution(4803104400186147350)
XLA Ops:
  0.0 90.8 %shard_map.55 = f32[128,3072]{1,0:T(8,128)} custom-call(bf16[3,128,3072]{2,1,0:T(8,128)(2,1)} %bitcast.1, f32[6]{0:T(128)} %eta_hbm.1, f32[6,64,64]{2,1,0:T(8,128)} %initial_hbm.1, f32[384]{0:T(512)} %gain_hbm.1, bf16[384,3072]{1,0:T(8,128)(2,1)} %w_hbm.1), custom_call_target="tpu_custom_call" | custom-call | tf_op jit(solution)/shard_map/pallas_call | solution.py:587
  90.8 2.7 %copy.7 = f32[128,3072]{1,0:T(8,128)} copy(f32[128,3072]{1,0:T(8,128)} %shard_map.55) | data formatting | bytes 3145728

commit v4 on v3

--- a/solution.py
+++ b/solution.py
@@ -122,23 +122,23 @@
             device_id=along(part, d), device_id_type=MESH,
         )
 
-    def band(part, d):
+    def band(part, d, side_half, core_base):
         last = z if part == 0 else y
-        at_rows, _ = piece(part, base, (last + side - d) % side, 0)
-        return whole.at[pl.ds(1, xs - 1), at_rows, :]
-
-    def w2_copy(part, d):
-        return pltpu.make_async_remote_copy(
-            src_ref=band(part, 0), dst_ref=band(part, 0),
-            send_sem=w2_send.at[part, d], recv_sem=w2_recv.at[part, d],
+        at_rows, _ = piece(part, core_base, (last + side - d) % side, 0)
+        return whole.at[pl.ds(1, xs - 1), at_rows, pl.ds(side_half * 2 * cols, 2 * cols)]
+
+    passed = {1: 0, 3: 1}
+
+    def w2_copy(part, d, order):
+        where = band(part, 0, passed[d] if order == 0 else 1 - passed[d], base)
+        return pltpu.make_async_remote_copy(
+            src_ref=where, dst_ref=where,
+            send_sem=w2_send.at[part, d, order], recv_sem=w2_recv.at[part, d, order],
             device_id=along(1 - part, d), device_id_type=MESH,
         )
 
     def w3_copy(part, d):
-        at_cols = pl.ds(0 if d == 1 else 2 * cols, 2 * cols)
-        last = z if part == 0 else y
-        at_rows, _ = piece(part, base, (last + side - d) % side, 0)
-        where = whole.at[pl.ds(1, xs - 1), at_rows, at_cols]
+        where = band(part, d, passed[d], base)
         return pltpu.make_async_remote_copy(
             src_ref=where, dst_ref=where,
             send_sem=w3_send.at[part, d], recv_sem=w3_recv.at[part, d],
@@ -147,16 +147,17 @@
 
     sibling = (s, x * 2 + 1 - c)
 
-    def sibling_band(part, d):
-        return pltpu.make_async_remote_copy(
-            src_ref=band(part, d), dst_ref=band(part, d),
-            send_sem=sib_send.at[part, d], recv_sem=sib_recv.at[part, d],
+    def sibling_band(part, d, side_half, core_base):
+        where = band(part, d, side_half, core_base)
+        return pltpu.make_async_remote_copy(
+            src_ref=where, dst_ref=where,
+            send_sem=sib_send.at[part, d, side_half], recv_sem=sib_recv.at[part, d, side_half],
             device_id=sibling, device_id_type=MESH,
         )
 
     sibling_own = pltpu.make_async_remote_copy(
         src_ref=w_hbm, dst_ref=whole.at[0, pl.ds(pl.multiple_of(base, PAIR), width), :],
-        send_sem=sib_send.at[2, 0], recv_sem=sib_recv.at[2, 0],
+        send_sem=sib_send.at[2, 0, 0], recv_sem=sib_recv.at[2, 0, 0],
         device_id=sibling, device_id_type=MESH,
     )
 
@@ -187,11 +188,15 @@
 
     kv_copy(1).start()
     for part in range(2):
-        for i in (1, 3, 2):
+        for i in (2, 1, 3):
             wx_copy(part, i).start()
-    for d in (2, 3, 6, 7):
-        kv_copy(d).start()
     q_copy(1).start()
+    kv_copy(2).start()
+    kv_copy(3).start()
+    kv_copy(6).start()
+    kv_copy(7).start()
+    kv_copy(4).start()
+    kv_copy(5).start()
 
     def near(i):
         return jnp.where(i < 2, i, xs + 1 - i)
@@ -217,10 +222,15 @@
 
         kv_copy(2 * dx + 1).wait_recv()
 
-        @pl.when(n == xs - 1)
-        def _():
-            for d in range(2, heads):
-                q_copy(d).start()
+        @pl.when(n == 1)
+        def _():
+            q_copy(4).start()
+            q_copy(5).start()
+            q_copy(2).start()
+            q_copy(3).start()
+            q_copy(6).start()
+            q_copy(7).start()
+
 
         first = {}
         for i in range(group_batches):
@@ -262,29 +272,22 @@
 
         @pl.when(n == 0)
         def _():
-            sibling_own.start()
             for part in range(2):
                 for i in range(1, xs):
                     wx_copy(part, i).wait_send()
-            for d in (4, 5):
-                kv_copy(d).start()
-            for part in range(2):
                 for i in range(1, xs):
                     wx_copy(part, i).wait_recv()
-            for part in range(2):
                 for d in (2, 1, 3):
                     w1_copy(part, d).start()
-
-        @pl.when(n == 2)
-        def _():
+            sibling_own.start()
             for part in range(2):
                 for d in (1, 2, 3):
                     w1_copy(part, d).wait_recv()
+                for d in (1, 3):
+                    w2_copy(part, d, 0).start()
             for part in range(2):
-                for d in (1, 3):
-                    w2_copy(part, d).start()
-            for part in range(2):
-                sibling_band(part, 0).start()
+                for side_half in range(2):
+                    sibling_band(part, 0, side_half, base).start()
 
     loop(0, xs, chip_maps)
 
@@ -338,6 +341,10 @@
 
     loop(1, seqs, send_total)
 
+    for part in range(2):
+        for d in (1, 3):
+            w2_copy(part, d, 1).start()
+
     def fin_copy(k, to):
         return pltpu.make_async_remote_copy(
             src_ref=outbox.at[to], dst_ref=entry.at[k],
@@ -426,6 +433,14 @@
         loop(1, seqs, lambda d: fin_copy(my_chain, (s + d) % seqs).start())
 
     multiply_queries(jnp.int32(xs // 2))
+
+    for part in range(2):
+        for d in (1, 3):
+            w2_copy(part, d, 0).wait_recv()
+            w3_copy(part, d).start()
+    for part in range(2):
+        for d in (1, 3):
+            sibling_band(part, d, passed[d], base).start()
 
     def wait_entry(k):
         @pl.when(chain_at(k) != s)
@@ -503,13 +518,12 @@
 
     for part in range(2):
         for d in (1, 3):
-            w2_copy(part, d).wait_recv()
-            w3_copy(part, d).start()
-            sibling_band(part, d).start()
+            w2_copy(part, d, 1).wait_recv()
+            sibling_band(part, d, 1 - passed[d], base).start()
     for part in range(2):
         for d in (1, 3):
             w3_copy(part, d).wait_recv()
-        sibling_band(part, 2).start()
+            sibling_band(part, 2, passed[d], base).start()
 
     own_w.wait()
     sibling_own.wait_recv()
@@ -517,19 +531,10 @@
     for d in range(1, heads):
         nrm_copy(d).wait_recv()
 
-    def sibling_arrival(part, d):
-        last = z if part == 0 else y
-        at_rows, _ = piece(part, width - base, (last + side - d) % side, 0)
-        where = whole.at[pl.ds(1, xs - 1), at_rows, :]
-        return pltpu.make_async_remote_copy(
-            src_ref=where, dst_ref=where,
-            send_sem=sib_send.at[part, d], recv_sem=sib_recv.at[part, d],
-            device_id=sibling, device_id_type=MESH,
-        )
-
     for part in range(2):
         for d in range(side):
-            sibling_arrival(part, d).wait_recv()
+            for side_half in range(2):
+                sibling_band(part, d, side_half, width - base).wait_recv()
 
     tile = 512
 
@@ -546,10 +551,12 @@
         for i in range(1, xs):
             w1_copy(part, i).wait_send()
         for d in (1, 3):
-            w2_copy(part, d).wait_send()
+            w2_copy(part, d, 0).wait_send()
+            w2_copy(part, d, 1).wait_send()
             w3_copy(part, d).wait_send()
         for d in range(side):
-            sibling_band(part, d).wait_send()
+            for side_half in range(2):
+                sibling_band(part, d, side_half, base).wait_send()
     sibling_own.wait_send()
 
     def drain_head(d):
@@ -582,7 +589,7 @@
     tokens = rows * heads
     batches = tokens // MB
     xs = heads // 2
-    anywhere = pl.BlockSpec(memory_space=pl.ANY)
+    anywhere = pl.BlockSpec(memory_space=pltpu.HBM)
     dma = pltpu.SemaphoreType.DMA
     return pl.pallas_call(
         functools.partial(layer_kernel, seqs, heads, pairs),
@@ -612,8 +619,8 @@
             dma((heads,)), dma((heads,)), dma((heads,)), dma((heads,)),
             dma((4 * pairs,)), dma((seqs,)), dma((seqs,)), dma((4 * pairs,)),
             dma((heads,)), dma((heads,)),
-            dma((2, 4)), dma((2, 4)), dma((2, 4)), dma((2, 4)), dma((2, 4)), dma((2, 4)),
-            dma((2, 4)), dma((2, 4)), dma((3, 4)), dma((3, 4)),
+            dma((2, 4)), dma((2, 4)), dma((2, 4)), dma((2, 4)), dma((2, 4, 2)), dma((2, 4, 2)),
+            dma((2, 4)), dma((2, 4)), dma((3, 4, 2)), dma((3, 4, 2)),
         ],
         compiler_params=pltpu.CompilerParams(
             collective_id=0, has_side_effects=True, vmem_limit_bytes=57 << 20

time: 93.6 us -> 80.4 us (0.86)
  Pallas kernels: 90.8 us -> 77.6 us
    pallas_call x1, Pallas kernels: 90.8 us -> 77.6 us  [layer(): pl.pallas_call(functools.partial(layer_kernel, seqs, heads, pairs), out_s...]
where the time goes in v4:
time: 80.4 us; the launch traced here: 80.3 us
  Pallas kernels  77.6 us (97%)
  local copies, waits for them, and re-layouts  2.7 us (3%)
    pallas_call x1, Pallas kernels, layer(): pl.pallas_call(functools.partial(layer_kernel, seqs, heads, pairs), out_s...  77.6 us
    unnamed x1, local copies, waits for them, and re-layouts  2.7 us

profile of v4, /device:TPU:1, one launch (start us, length us, event | category | flops | bytes accessed | tf_op | source)
XLA Modules:
  0.0 80.3 jit_solution(15352307692246977712)
XLA Ops:
  0.0 77.6 %shard_map.55 = f32[128,3072]{1,0:T(8,128)} custom-call(bf16[3,128,3072]{2,1,0:T(8,128)(2,1)} %bitcast.1, f32[6]{0:T(128)} %eta_hbm.1, f32[6,64,64]{2,1,0:T(8,128)} %initial_hbm.1, f32[384]{0:T(512)} %gain_hbm.1, bf16[384,3072]{1,0:T(8,128)(2,1)} %w_hbm.1), custom_call_target="tpu_custom_call" | custom-call | tf_op jit(solution)/shard_map/pallas_call | solution.py:594
  77.6 2.7 %copy.7 = f32[128,3072]{1,0:T(8,128)} copy(f32[128,3072]{1,0:T(8,128)} %shard_map.55) | data formatting | bytes 3145728

commit v5 on v4

--- a/solution.py
+++ b/solution.py
@@ -94,31 +94,34 @@
     step = half // side
     cols = w_hbm.shape[1] // side
 
-    def piece(part, first, last, second):
+    def piece(part, first, last, second, k=0):
         at = part * half + last * step
-        return pl.ds(pl.multiple_of(first + at, 16), step), pl.ds(pl.multiple_of(second * cols, PAIR), cols)
-
-    def wx_copy(part, i):
+        return (
+            pl.ds(pl.multiple_of(first + at, 16), step),
+            pl.ds(pl.multiple_of((2 * second + k) * (cols // 2), PAIR), cols // 2),
+        )
+
+    def wx_copy(part, i, k):
         last, second = (z, y) if part == 0 else (y, z)
-        from_rows, at_cols = piece(part, 0, last, second)
-        to_rows, _ = piece(part, base, last, second)
+        from_rows, at_cols = piece(part, 0, last, second, k)
+        to_rows, _ = piece(part, base, last, second, k)
         return pltpu.make_async_remote_copy(
             src_ref=w_hbm.at[from_rows, at_cols],
             dst_ref=whole.at[i, to_rows, at_cols],
-            send_sem=wx_send.at[part, i], recv_sem=wx_recv.at[part, i],
+            send_sem=wx_send.at[part, i, k], recv_sem=wx_recv.at[part, i, k],
             device_id=(s, ((x + xs - i) % xs) * 2 + c), device_id_type=MESH,
         )
 
     def along(axis, d):
         return (z * side + (y + d) % side, h) if axis == 0 else (((z + d) % side) * side + y, h)
 
-    def w1_copy(part, d):
+    def w1_copy(part, d, k):
         last, second = (z, y) if part == 0 else (y, z)
-        at_rows, at_cols = piece(part, base, last, second)
+        at_rows, at_cols = piece(part, base, last, second, k)
         where = whole.at[pl.ds(1, xs - 1), at_rows, at_cols]
         return pltpu.make_async_remote_copy(
             src_ref=where, dst_ref=where,
-            send_sem=w1_send.at[part, d], recv_sem=w1_recv.at[part, d],
+            send_sem=w1_send.at[part, d, k], recv_sem=w1_recv.at[part, d, k],
             device_id=along(part, d), device_id_type=MESH,
         )
 
@@ -130,7 +133,12 @@
     passed = {1: 0, 3: 1}
 
     def w2_copy(part, d, order):
-        where = band(part, 0, passed[d] if order == 0 else 1 - passed[d], base)
+        if order == 0:
+            where = band(part, 0, passed[d], base)
+        else:
+            at_rows, _ = piece(part, base, z if part == 0 else y, 0)
+            at_cols = pl.ds((2 * (1 - passed[d]) + order - 1) * cols, cols)
+            where = whole.at[pl.ds(1, xs - 1), at_rows, at_cols]
         return pltpu.make_async_remote_copy(
             src_ref=where, dst_ref=where,
             send_sem=w2_send.at[part, d, order], recv_sem=w2_recv.at[part, d, order],
@@ -187,9 +195,10 @@
         lax.fori_loop(first, last, run, 0)
 
     kv_copy(1).start()
-    for part in range(2):
-        for i in (2, 1, 3):
-            wx_copy(part, i).start()
+    for k in range(2):
+        for part in range(2):
+            for i in (2, 1, 3):
+                wx_copy(part, i, k).start()
     q_copy(1).start()
     kv_copy(2).start()
     kv_copy(3).start()
@@ -272,19 +281,22 @@
 
         @pl.when(n == 0)
         def _():
-            for part in range(2):
-                for i in range(1, xs):
-                    wx_copy(part, i).wait_send()
-                for i in range(1, xs):
-                    wx_copy(part, i).wait_recv()
-                for d in (2, 1, 3):
-                    w1_copy(part, d).start()
+            for k in range(2):
+                for part in range(2):
+                    for i in range(1, xs):
+                        wx_copy(part, i, k).wait_recv()
+                    for d in (2, 1, 3):
+                        w1_copy(part, d, k).start()
             sibling_own.start()
             for part in range(2):
                 for d in (1, 2, 3):
-                    w1_copy(part, d).wait_recv()
+                    for k in range(2):
+                        w1_copy(part, d, k).wait_recv()
                 for d in (1, 3):
                     w2_copy(part, d, 0).start()
+            for part in range(2):
+                for d in (1, 3):
+                    w2_copy(part, d, 1).start()
             for part in range(2):
                 for side_half in range(2):
                     sibling_band(part, 0, side_half, base).start()
@@ -343,7 +355,7 @@
 
     for part in range(2):
         for d in (1, 3):
-            w2_copy(part, d, 1).start()
+            w2_copy(part, d, 2).start()
 
     def fin_copy(k, to):
         return pltpu.make_async_remote_copy(
@@ -519,6 +531,7 @@
     for part in range(2):
         for d in (1, 3):
             w2_copy(part, d, 1).wait_recv()
+            w2_copy(part, d, 2).wait_recv()
             sibling_band(part, d, 1 - passed[d], base).start()
     for part in range(2):
         for d in (1, 3):
@@ -549,10 +562,13 @@
 
     for part in range(2):
         for i in range(1, xs):
-            w1_copy(part, i).wait_send()
+            for k in range(2):
+                wx_copy(part, i, k).wait_send()
+                w1_copy(part, i, k).wait_send()
         for d in (1, 3):
             w2_copy(part, d, 0).wait_send()
             w2_copy(part, d, 1).wait_send()
+            w2_copy(part, d, 2).wait_send()
             w3_copy(part, d).wait_send()
         for d in range(side):
             for side_half in range(2):
@@ -619,11 +635,11 @@
             dma((heads,)), dma((heads,)), dma((heads,)), dma((heads,)),
             dma((4 * pairs,)), dma((seqs,)), dma((seqs,)), dma((4 * pairs,)),
             dma((heads,)), dma((heads,)),
-            dma((2, 4)), dma((2, 4)), dma((2, 4)), dma((2, 4)), dma((2, 4, 2)), dma((2, 4, 2)),
+            dma((2, 4, 2)), dma((2, 4, 2)), dma((2, 4, 2)), dma((2, 4, 2)), dma((2, 4, 3)), dma((2, 4, 3)),
             dma((2, 4)), dma((2, 4)), dma((3, 4, 2)), dma((3, 4, 2)),
         ],
         compiler_params=pltpu.CompilerParams(
-            collective_id=0, has_side_effects=True, vmem_limit_bytes=57 << 20
+            collective_id=0, has_side_effects=True, vmem_limit_bytes=50 << 20
         ),
     )(qkv, eta, initial, gain, w_out)
 

time: 80.4 us -> 77.2 us (0.960)
  Pallas kernels: 77.6 us -> 73.6 us
    pallas_call x1, Pallas kernels: 77.6 us -> 73.6 us  [layer(): pl.pallas_call(functools.partial(layer_kernel, seqs, heads, pairs), out_s...]
    unnamed x1 -> x7, local copies, waits for them, and re-layouts: 2.7 us -> 3.41 us
where the time goes in v5:
time: 77.2 us; the launch traced here: 77 us
  Pallas kernels  73.6 us (95%)
  local copies, waits for them, and re-layouts  3.41 us (4%)
    pallas_call x1, Pallas kernels, layer(): pl.pallas_call(functools.partial(layer_kernel, seqs, heads, pairs), out_s...  73.6 us
    unnamed x7, local copies, waits for them, and re-layouts  3.41 us

profile of v5, /device:TPU:1, one launch (start us, length us, event | category | flops | bytes accessed | tf_op | source)
XLA Modules:
  0.0 77.0 jit_solution(6440043406633377309)
XLA Ops:
  0.0 0.0 copy-start
  0.0 0.9 %copy-done = f32[6,64,64]{2,1,0:T(8,128)S(1)} copy-done((f32[6,64,64]{2,1,0:T(8,128)S(1)}, f32[6,64,64]{2,1,0:T(8,128)}, u32[]{:S(2)}) %copy-start) | copy-done | bytes 98328
  0.9 0.0 copy-start.1
  0.9 0.7 copy-done.1
  1.6 0.0 copy-start.2
  1.6 0.7 copy-done.2
  2.3 73.6 %shard_map.55 = f32[128,3072]{1,0:T(8,128)S(1)} custom-call(bf16[3,128,3072]{2,1,0:T(8,128)(2,1)} %bitcast.1, f32[6]{0:T(128)S(1)} %copy-done.2, f32[6,64,64]{2,1,0:T(8,128)S(1)} %copy-done, f32[384]{0:T(512)S(1)} %copy-done.1, bf16[384,3072]{1,0:T(8,128)(2,1)} %w_hbm.1), custom_call_target="tpu_custom_call" | custom-call | tf_op jit(solution)/shard_map/pallas_call | solution.py:610
  75.9 1.1 %copy.7 = f32[128,3072]{1,0:T(8,128)} copy(f32[128,3072]{1,0:T(8,128)S(1)} %shard_map.55) | data formatting | bytes 3145728
Async XLA Ops:
  0.0 0.9 %copy-start = (f32[6,64,64]{2,1,0:T(8,128)S(1)}, f32[6,64,64]{2,1,0:T(8,128)}, u32[]{:S(2)}) copy-start(f32[6,64,64]{2,1,0:T(8,128)} %initial_hbm.1) | copy-start | bytes 294916
  0.9 0.7 copy-start.1
  1.6 0.7 copy-start.2

commit v6 on v5

--- a/solution.py
+++ b/solution.py
@@ -33,9 +33,10 @@
     seqs, heads, pairs,
     qkv, eta_hbm, initial_hbm, gain_hbm, w_hbm, out,
     eta, initial, gain, recv, a_ref, b_ref, pre, group, totals, inbox, outbox, entry,
-    q_high, q_low, r_ref, normed, normed_in, whole,
+    q_high, q_low, r_ref, normed, normed_in, whole, mixed,
     const_sem, own_sem, kv_send, kv_recv, q_send, q_recv, tot_send, tot_recv, fin_send, fin_recv, nrm_send, nrm_recv,
-    wx_send, wx_recv, w1_send, w1_recv, w2_send, w2_recv, w3_send, w3_recv, sib_send, sib_recv,
+    wx_send, wx_recv, w1_send, w1_recv, w2_send, w2_recv, w3_send, w3_recv, sib_send, sib_recv, last_send, last_recv,
+    out_sem, wd_send, wd_recv, direct_send, direct_recv,
 ):
     s = lax.axis_index("seq")
     h = lax.axis_index("head")
@@ -145,11 +146,32 @@
             device_id=along(1 - part, d), device_id_type=MESH,
         )
 
-    def w3_copy(part, d):
-        where = band(part, d, passed[d], base)
+    def quarter(part, d, side_half, k, core_base):
+        last = z if part == 0 else y
+        at_rows, _ = piece(part, core_base, (last + side - d) % side, 0)
+        at_cols = pl.ds((2 * side_half + k) * cols, cols if k == 0 else cols // 2)
+        return whole.at[pl.ds(1, xs - 1), at_rows, at_cols]
+
+    def left_over(part, side_half, core_base):
+        last = z if part == 0 else y
+        at_rows, _ = piece(part, core_base, (last + 2) % side, 0)
+        return at_rows, pl.ds((2 * side_half + 1) * cols + cols // 2, cols // 2)
+
+    def wd_copy(part, side_half, i):
+        from_rows, at_cols = left_over(part, side_half, 0)
+        to_rows, _ = left_over(part, side_half, base)
+        return pltpu.make_async_remote_copy(
+            src_ref=w_hbm.at[from_rows, at_cols],
+            dst_ref=whole.at[i, to_rows, at_cols],
+            send_sem=wd_send.at[part, side_half, i], recv_sem=wd_recv.at[part, side_half, i],
+            device_id=(s, ((x + xs - i) % xs) * 2 + c), device_id_type=MESH,
+        )
+
+    def w3_copy(part, d, k):
+        where = quarter(part, d, passed[d], k, base)
         return pltpu.make_async_remote_copy(
             src_ref=where, dst_ref=where,
-            send_sem=w3_send.at[part, d], recv_sem=w3_recv.at[part, d],
+            send_sem=w3_send.at[part, d, k], recv_sem=w3_recv.at[part, d, k],
             device_id=along(1 - part, d), device_id_type=MESH,
         )
 
@@ -160,6 +182,23 @@
         return pltpu.make_async_remote_copy(
             src_ref=where, dst_ref=where,
             send_sem=sib_send.at[part, d, side_half], recv_sem=sib_recv.at[part, d, side_half],
+            device_id=sibling, device_id_type=MESH,
+        )
+
+    def sibling_quarter(part, d, k, core_base):
+        where = quarter(part, 2, passed[d], k, core_base)
+        return pltpu.make_async_remote_copy(
+            src_ref=where, dst_ref=where,
+            send_sem=last_send.at[part, d, k], recv_sem=last_recv.at[part, d, k],
+            device_id=sibling, device_id_type=MESH,
+        )
+
+    def sibling_direct(part, side_half, core_base):
+        at_rows, at_cols = left_over(part, side_half, core_base)
+        where = whole.at[pl.ds(1, xs - 1), at_rows, at_cols]
+        return pltpu.make_async_remote_copy(
+            src_ref=where, dst_ref=where,
+            send_sem=direct_send.at[part, side_half], recv_sem=direct_recv.at[part, side_half],
             device_id=sibling, device_id_type=MESH,
         )
 
@@ -239,6 +278,10 @@
             q_copy(3).start()
             q_copy(6).start()
             q_copy(7).start()
+            for part in range(2):
+                for side_half in range(2):
+                    for i in (2, 1, 3):
+                        wd_copy(part, side_half, i).start()
 
 
         first = {}
@@ -295,9 +338,6 @@
                 for d in (1, 3):
                     w2_copy(part, d, 0).start()
             for part in range(2):
-                for d in (1, 3):
-                    w2_copy(part, d, 1).start()
-            for part in range(2):
                 for side_half in range(2):
                     sibling_band(part, 0, side_half, base).start()
 
@@ -355,7 +395,8 @@
 
     for part in range(2):
         for d in (1, 3):
-            w2_copy(part, d, 2).start()
+            w2_copy(part, d, 1).start()
+
 
     def fin_copy(k, to):
         return pltpu.make_async_remote_copy(
@@ -448,8 +489,15 @@
 
     for part in range(2):
         for d in (1, 3):
+            w2_copy(part, d, 2).start()
+
+    for part in range(2):
+        for d in (1, 3):
             w2_copy(part, d, 0).wait_recv()
-            w3_copy(part, d).start()
+            w3_copy(part, d, 0).start()
+    for part in range(2):
+        for d in (1, 3):
+            w3_copy(part, d, 1).start()
     for part in range(2):
         for d in (1, 3):
             sibling_band(part, d, passed[d], base).start()
@@ -534,9 +582,15 @@
             w2_copy(part, d, 2).wait_recv()
             sibling_band(part, d, 1 - passed[d], base).start()
     for part in range(2):
-        for d in (1, 3):
-            w3_copy(part, d).wait_recv()
-            sibling_band(part, 2, passed[d], base).start()
+        for side_half in range(2):
+            for i in range(1, xs):
+                wd_copy(part, side_half, i).wait_recv()
+            sibling_direct(part, side_half, base).start()
+    for k in range(2):
+        for part in range(2):
+            for d in (1, 3):
+                w3_copy(part, d, k).wait_recv()
+                sibling_quarter(part, d, k, base).start()
 
     own_w.wait()
     sibling_own.wait_recv()
@@ -544,21 +598,31 @@
     for d in range(1, heads):
         nrm_copy(d).wait_recv()
 
-    for part in range(2):
-        for d in range(side):
-            for side_half in range(2):
-                sibling_band(part, d, side_half, width - base).wait_recv()
-
-    tile = 512
-
-    def project(j):
-        at = pl.ds(pl.multiple_of(j * tile, tile), tile)
-        total = dot(normed_in[0], whole[0, :, at])
-        for i in range(1, xs):
-            total = total + dot(normed_in[i], whole[i, :, at])
-        out[:, at] = total
-
-    loop(0, w_hbm.shape[1] // tile, project)
+    outgoing = []
+    for k in range(2):
+        if k == 0:
+            for part in range(2):
+                for d in (0, 1, 3):
+                    for side_half in range(2):
+                        sibling_band(part, d, side_half, width - base).wait_recv()
+                for side_half in range(2):
+                    sibling_direct(part, side_half, width - base).wait_recv()
+        for part in range(2):
+            for d in (1, 3):
+                sibling_quarter(part, d, k, width - base).wait_recv()
+
+        def project(side_half):
+            at = pl.ds(pl.multiple_of((2 * side_half + k) * cols, PAIR), cols)
+            total = dot(normed_in[0], whole[0, :, at])
+            for i in range(1, xs):
+                total = total + dot(normed_in[i], whole[i, :, at])
+            mixed[2 * side_half + k] = total
+            pltpu.make_async_copy(mixed.at[2 * side_half + k], out.at[:, at], out_sem.at[2 * side_half + k]).start()
+
+        loop(0, 2, project)
+
+    for j in range(side):
+        pltpu.make_async_copy(mixed.at[j], out.at[:, pl.ds(j * cols, cols)], out_sem.at[j]).wait()
 
     for part in range(2):
         for i in range(1, xs):
@@ -569,8 +633,14 @@
             w2_copy(part, d, 0).wait_send()
             w2_copy(part, d, 1).wait_send()
             w2_copy(part, d, 2).wait_send()
-            w3_copy(part, d).wait_send()
-        for d in range(side):
+            for k in range(2):
+                w3_copy(part, d, k).wait_send()
+                sibling_quarter(part, d, k, base).wait_send()
+        for side_half in range(2):
+            for i in range(1, xs):
+                wd_copy(part, side_half, i).wait_send()
+            sibling_direct(part, side_half, base).wait_send()
+        for d in (0, 1, 3):
             for side_half in range(2):
                 sibling_band(part, d, side_half, base).wait_send()
     sibling_own.wait_send()
@@ -611,7 +681,7 @@
         functools.partial(layer_kernel, seqs, heads, pairs),
         out_shape=jax.ShapeDtypeStruct((rows, columns), F32),
         in_specs=[anywhere] * 5,
-        out_specs=pl.BlockSpec(memory_space=pltpu.VMEM),
+        out_specs=anywhere,
         scratch_shapes=[
             pltpu.SMEM(eta.shape, F32),
             pltpu.VMEM(initial.shape, F32),
@@ -631,15 +701,17 @@
             pltpu.VMEM((tokens, width), BF),
             pltpu.VMEM((xs, rows, 2 * width), BF),
             pltpu.VMEM((xs, 2 * width, columns), BF),
+            pltpu.VMEM((4, rows, columns // 4), F32),
             dma((3,)), dma((4,)),
             dma((heads,)), dma((heads,)), dma((heads,)), dma((heads,)),
             dma((4 * pairs,)), dma((seqs,)), dma((seqs,)), dma((4 * pairs,)),
             dma((heads,)), dma((heads,)),
             dma((2, 4, 2)), dma((2, 4, 2)), dma((2, 4, 2)), dma((2, 4, 2)), dma((2, 4, 3)), dma((2, 4, 3)),
-            dma((2, 4)), dma((2, 4)), dma((3, 4, 2)), dma((3, 4, 2)),
+            dma((2, 4, 2)), dma((2, 4, 2)), dma((3, 4, 2)), dma((3, 4, 2)), dma((2, 4, 2)), dma((2, 4, 2)),
+            dma((4,)), dma((2, 2, 4)), dma((2, 2, 4)), dma((2, 2)), dma((2, 2)),
         ],
         compiler_params=pltpu.CompilerParams(
-            collective_id=0, has_side_effects=True, vmem_limit_bytes=50 << 20
+            collective_id=0, has_side_effects=True, vmem_limit_bytes=57 << 20
         ),
     )(qkv, eta, initial, gain, w_out)
 

time: 77.2 us -> 74.7 us (0.968)
  Pallas kernels: 73.6 us -> 71.9 us
    pallas_call x1, Pallas kernels: 73.6 us -> 71.9 us  [layer(): pl.pallas_call(functools.partial(layer_kernel, seqs, heads, pairs), out_s...]
    unnamed x7 -> x1, local copies, waits for them, and re-layouts: 3.41 us -> 2.7 us
where the time goes in v6:
time: 74.7 us; the launch traced here: 74.6 us
  Pallas kernels  71.9 us (96%)
  local copies, waits for them, and re-layouts  2.7 us (4%)
    pallas_call x1, Pallas kernels, layer(): pl.pallas_call(functools.partial(layer_kernel, seqs, heads, pairs), out_s...  71.9 us
    unnamed x1, local copies, waits for them, and re-layouts  2.7 us

profile of v6, /device:TPU:1, one launch (start us, length us, event | category | flops | bytes accessed | tf_op | source)
XLA Modules:
  0.0 74.6 jit_solution(440794299344914321)
XLA Ops:
  0.0 71.9 %shard_map.55 = f32[128,3072]{1,0:T(8,128)} custom-call(bf16[3,128,3072]{2,1,0:T(8,128)(2,1)} %bitcast.1, f32[6]{0:T(128)} %eta_hbm.1, f32[6,64,64]{2,1,0:T(8,128)} %initial_hbm.1, f32[384]{0:T(512)} %gain_hbm.1, bf16[384,3072]{1,0:T(8,128)(2,1)} %w_hbm.1), custom_call_target="tpu_custom_call" | custom-call | tf_op jit(solution)/shard_map/pallas_call | solution.py:680
  71.9 2.7 %copy.7 = f32[128,3072]{1,0:T(8,128)} copy(f32[128,3072]{1,0:T(8,128)} %shard_map.55) | data formatting | bytes 3145728

commit v7 on v6

--- a/solution.py
+++ b/solution.py
@@ -36,7 +36,7 @@
     q_high, q_low, r_ref, normed, normed_in, whole, mixed,
     const_sem, own_sem, kv_send, kv_recv, q_send, q_recv, tot_send, tot_recv, fin_send, fin_recv, nrm_send, nrm_recv,
     wx_send, wx_recv, w1_send, w1_recv, w2_send, w2_recv, w3_send, w3_recv, sib_send, sib_recv, last_send, last_recv,
-    out_sem, wd_send, wd_recv, direct_send, direct_recv,
+    plane, out_sem, wd_send, wd_recv, direct_send, direct_recv,
 ):
     s = lax.axis_index("seq")
     h = lax.axis_index("head")
@@ -56,12 +56,13 @@
         pl.semaphore_signal(barrier, inc=1, device_id=(s, (h + d) % heads), device_id_type=MESH)
         return 0
 
-    def greet_seq(d, _):
-        pl.semaphore_signal(barrier, inc=1, device_id=((s + d) % seqs, h), device_id_type=MESH)
+    def greet_sides(d, _):
+        pl.semaphore_signal(barrier, inc=1, device_id=(z * side + (y + d) % side, h), device_id_type=MESH)
+        pl.semaphore_signal(barrier, inc=1, device_id=(((z + d) % side) * side + y, h), device_id_type=MESH)
         return 0
 
+    lax.fori_loop(1, side, greet_sides, 0)
     lax.fori_loop(1, heads, greet_head, 0)
-    lax.fori_loop(1, seqs, greet_seq, 0)
 
     constants = [
         pltpu.make_async_copy(eta_hbm, eta, const_sem.at[0]),
@@ -85,7 +86,13 @@
     base = c * width
     own_w = pltpu.make_async_copy(w_hbm, whole.at[0, pl.ds(pl.multiple_of(base, PAIR), width), :], own_sem.at[2])
     own_w.start()
-    pl.semaphore_wait(barrier, heads + seqs - 2)
+    pl.semaphore_wait(barrier, heads - 1 + 2 * (side - 1))
+
+    def tell(d, _):
+        pl.semaphore_signal(plane, inc=1, device_id=(z * side + (y + d) % side, h), device_id_type=MESH)
+        return 0
+
+    lax.fori_loop(1, side, tell, 0)
 
     def peer(d, sign):
         dx, dc = d // 2, d % 2
@@ -149,13 +156,13 @@
     def quarter(part, d, side_half, k, core_base):
         last = z if part == 0 else y
         at_rows, _ = piece(part, core_base, (last + side - d) % side, 0)
-        at_cols = pl.ds((2 * side_half + k) * cols, cols if k == 0 else cols // 2)
+        at_cols = pl.ds((2 * side_half + k) * cols, cols if k == 0 else cols // 3)
         return whole.at[pl.ds(1, xs - 1), at_rows, at_cols]
 
     def left_over(part, side_half, core_base):
         last = z if part == 0 else y
         at_rows, _ = piece(part, core_base, (last + 2) % side, 0)
-        return at_rows, pl.ds((2 * side_half + 1) * cols + cols // 2, cols // 2)
+        return at_rows, pl.ds((2 * side_half + 1) * cols + cols // 3, cols - cols // 3)
 
     def wd_copy(part, side_half, i):
         from_rows, at_cols = left_over(part, side_half, 0)
@@ -391,6 +398,7 @@
         def _():
             tot_copy(k).start()
 
+    pl.semaphore_wait(plane, side - 1)
     loop(1, seqs, send_total)
 
     for part in range(2):
@@ -595,7 +603,13 @@
     own_w.wait()
     sibling_own.wait_recv()
     own_normed.wait()
-    for d in range(1, heads):
+    nrm_copy(1).wait_recv()
+
+    def project_own(j):
+        mixed[j] = dot(normed_in[0], whole[0, :, pl.ds(pl.multiple_of(j * cols, PAIR), cols)])
+
+    loop(0, side, project_own)
+    for d in range(2, heads):
         nrm_copy(d).wait_recv()
 
     outgoing = []
@@ -613,7 +627,7 @@
 
         def project(side_half):
             at = pl.ds(pl.multiple_of((2 * side_half + k) * cols, PAIR), cols)
-            total = dot(normed_in[0], whole[0, :, at])
+            total = mixed[2 * side_half + k]
             for i in range(1, xs):
                 total = total + dot(normed_in[i], whole[i, :, at])
             mixed[2 * side_half + k] = total
@@ -708,7 +722,7 @@
             dma((heads,)), dma((heads,)),
             dma((2, 4, 2)), dma((2, 4, 2)), dma((2, 4, 2)), dma((2, 4, 2)), dma((2, 4, 3)), dma((2, 4, 3)),
             dma((2, 4, 2)), dma((2, 4, 2)), dma((3, 4, 2)), dma((3, 4, 2)), dma((2, 4, 2)), dma((2, 4, 2)),
-            dma((4,)), dma((2, 2, 4)), dma((2, 2, 4)), dma((2, 2)), dma((2, 2)),
+            pltpu.SemaphoreType.REGULAR, dma((4,)), dma((2, 2, 4)), dma((2, 2, 4)), dma((2, 2)), dma((2, 2)),
         ],
         compiler_params=pltpu.CompilerParams(
             collective_id=0, has_side_effects=True, vmem_limit_bytes=57 << 20

time: 74.7 us -> 73.7 us (0.987)
  Pallas kernels: 71.9 us -> 70.8 us
    pallas_call x1, Pallas kernels: 71.9 us -> 70.8 us  [layer(): pl.pallas_call(functools.partial(layer_kernel, seqs, heads, pairs), out_s...]
where the time goes in v7:
time: 73.7 us; the launch traced here: 73.5 us
  Pallas kernels  70.8 us (96%)
  local copies, waits for them, and re-layouts  2.7 us (4%)
    pallas_call x1, Pallas kernels, layer(): pl.pallas_call(functools.partial(layer_kernel, seqs, heads, pairs), out_s...  70.8 us
    unnamed x1, local copies, waits for them, and re-layouts  2.7 us

profile of v7, /device:TPU:1, one launch (start us, length us, event | category | flops | bytes accessed | tf_op | source)
XLA Modules:
  0.0 73.5 jit_solution(11264585432001165176)
XLA Ops:
  0.0 70.8 %shard_map.55 = f32[128,3072]{1,0:T(8,128)} custom-call(bf16[3,128,3072]{2,1,0:T(8,128)(2,1)} %bitcast.1, f32[6]{0:T(128)} %eta_hbm.1, f32[6,64,64]{2,1,0:T(8,128)} %initial_hbm.1, f32[384]{0:T(512)} %gain_hbm.1, bf16[384,3072]{1,0:T(8,128)(2,1)} %w_hbm.1), custom_call_target="tpu_custom_call" | custom-call | tf_op jit(solution)/shard_map/pallas_call | solution.py:694
  70.8 2.7 %copy.7 = f32[128,3072]{1,0:T(8,128)} copy(f32[128,3072]{1,0:T(8,128)} %shard_map.55) | data formatting | bytes 3145728

commit v8 on v7

--- a/solution.py
+++ b/solution.py
@@ -279,12 +279,12 @@
 
         @pl.when(n == 1)
         def _():
-            q_copy(4).start()
-            q_copy(5).start()
             q_copy(2).start()
             q_copy(3).start()
             q_copy(6).start()
             q_copy(7).start()
+            q_copy(4).start()
+            q_copy(5).start()
             for part in range(2):
                 for side_half in range(2):
                     for i in (2, 1, 3):

time: 73.7 us -> 73.1 us (level)
  no operation moved by 1% of the time
where the time goes in v8:
time: 73.1 us; the launch traced here: 72.9 us
  Pallas kernels  70.2 us (96%)
  local copies, waits for them, and re-layouts  2.7 us (4%)
    pallas_call x1, Pallas kernels, layer(): pl.pallas_call(functools.partial(layer_kernel, seqs, heads, pairs), out_s...  70.2 us
    unnamed x1, local copies, waits for them, and re-layouts  2.7 us

profile of v8, /device:TPU:1, one launch (start us, length us, event | category | flops | bytes accessed | tf_op | source)
XLA Modules:
  0.0 72.9 jit_solution(9404135504423143997)
XLA Ops:
  0.0 70.2 %shard_map.55 = f32[128,3072]{1,0:T(8,128)} custom-call(bf16[3,128,3072]{2,1,0:T(8,128)(2,1)} %bitcast.1, f32[6]{0:T(128)} %eta_hbm.1, f32[6,64,64]{2,1,0:T(8,128)} %initial_hbm.1, f32[384]{0:T(512)} %gain_hbm.1, bf16[384,3072]{1,0:T(8,128)(2,1)} %w_hbm.1), custom_call_target="tpu_custom_call" | custom-call | tf_op jit(solution)/shard_map/pallas_call | solution.py:694
  70.2 2.7 %copy.7 = f32[128,3072]{1,0:T(8,128)} copy(f32[128,3072]{1,0:T(8,128)} %shard_map.55) | data formatting | bytes 3145728
